TPU v7x, 32 devices: a whole 2x2x4 slice. The times are simulated.
32 devices in a mesh: row: 8 (over y, x, core), col: 4 (over z).
Axes of the slice: x: 2, y: 2, z: 4, core: 2. Of those that a mesh axis runs over, the one named last changes fastest.
Arguments:
- documents: bfloat16 [2, 4096, 2048], P(None, ('row', 'col')), may hold values from -6 to 6
- targets: bfloat16 [2, 4096, 2048], P(None, ('row', 'col')), may hold values from -6 to 6
- routes: int32 [2, 4096, 1], P(None, ('row', 'col')), may hold values from 0 to 31; in each aligned block of 128 rows (0 to 127, 128 to 255, ..., all dimensions but the last counted through in order) at most 8 rows name the same one
- doc_counts: int32 [8, 4], replicated, may hold values from 1 to 64
- module_one: float32 [8, 2048, 2048], P('row', 'col'), may hold values from -6 to 6
- module_two: float32 [4, 2048, 2048], P('col', 'row'), may hold values from -6 to 6
- moment_one: float32 [8, 2048, 2048], P('row', 'col'), may hold values from -0.75 to 0.75
- moment_two: float32 [4, 2048, 2048], P('col', 'row'), may hold values from -0.75 to 0.75
Outputs:
- new_one: float32 [8, 2048, 2048], P('row', 'col')
- new_two: float32 [4, 2048, 2048], P('col', 'row')
- next_moment_one: float32 [8, 2048, 2048], P('row', 'col')
- next_moment_two: float32 [4, 2048, 2048], P('col', 'row')
Inputs may be any that keep to these rules, and one draw needn't show every extreme that they name: `routes`: in each micro-batch, at most 8 of the 128 rows that one device holds name the same path.
All inputs are finite; a program needn't handle non-finite values.
Results may differ from a plain program's by a relative error of at most 0.011.
Values may be sent and summed in bfloat16 or wider, within the bound.
No kernel may reach another device: no remote copies, remote signals or barrier semaphores. Data moves between devices by JAX's collectives and lax.ppermute only.
A program may use at most 192 MiB of HBM per device.

v0:
```python
import jax
import jax.numpy as jnp
from jax import lax
from jax.sharding import PartitionSpec as P

D = 2048


beta_one = 0.9
beta_two = 0.95
inner_rate = 0.1
decay = 0.1
outer_rate = 0.7
outer_moment = 0.9


def silu_slope(pre):
    sig = jax.nn.sigmoid(pre)
    return sig * (1.0 + pre * (1.0 - sig))


def gradients(w_one, w_two, rows, targs, valid, rows_dev):
    scale = D ** (-0.5)
    pre = jnp.dot(rows, w_one, preferred_element_type=jnp.float32) * scale
    hidden = jax.nn.silu(pre).astype(jnp.bfloat16)
    out = (
        rows.astype(jnp.float32)
        + jnp.dot(hidden, w_two, preferred_element_type=jnp.float32) * scale
    )
    error = ((out - targs.astype(jnp.float32)) * valid / rows_dev).astype(jnp.bfloat16)
    grad_two = (
        lax.dot_general(hidden, error, (((0,), (0,)), ((), ())), preferred_element_type=jnp.float32)
        * scale
    )
    back = (
        lax.dot_general(error, w_two, (((1,), (1,)), ((), ())), preferred_element_type=jnp.float32)
        * scale
    )
    inner = (back * silu_slope(pre)).astype(jnp.bfloat16)
    grad_one = (
        lax.dot_general(rows, inner, (((0,), (0,)), ((), ())), preferred_element_type=jnp.float32)
        * scale
    )
    return (grad_one, grad_two)


def adamw(param, grad, first, second, step, guard):
    first = beta_one * first + (1.0 - beta_one) * grad
    second = beta_two * second + (1.0 - beta_two) * grad * grad
    fix_one = 1.0 - beta_one ** (step + 1)
    fix_two = 1.0 - beta_two ** (step + 1)
    update = first / fix_one / (jnp.sqrt(second / fix_two) + guard) + decay * param
    return (param - inner_rate * update, first, second)


def rounded(value):
    return lax.optimization_barrier(value.astype(jnp.bfloat16)).astype(jnp.float32)


def shards(documents, targets, routes, doc_counts, module_one, module_two, moment_one, moment_two):
    n_row = lax.axis_size("row")
    n_col = lax.axis_size("col")
    paths = n_row * n_col
    row_id = lax.axis_index("row")
    col_id = lax.axis_index("col")
    micro, rows_dev, width = documents.shape
    room = max(2, 2 * rows_dev // paths)
    slots_all = paths * micro * room
    guard = 0.5 / (D * rows_dev) ** 0.5
    dest = routes[:, :, 0]
    hit = (dest[:, :, None] == jnp.arange(paths, dtype=jnp.int32)[None, None, :]).astype(jnp.int32)
    before = jnp.cumsum(hit, axis=1) - hit
    slot_rank = jnp.sum(before * hit, axis=2)
    micro_ids = jnp.arange(micro, dtype=jnp.int32)[:, None]
    target_slot = dest * (micro * room) + micro_ids * room + slot_rank
    place = (
        target_slot[:, :, None] == jnp.arange(slots_all, dtype=jnp.int32)[None, None, :]
    ).astype(jnp.bfloat16)
    sent_docs = jnp.einsum(
        "mrs,mrd->sd", place, documents, preferred_element_type=jnp.float32
    ).astype(jnp.bfloat16)
    sent_targs = jnp.einsum(
        "mrs,mrd->sd", place, targets, preferred_element_type=jnp.float32
    ).astype(jnp.bfloat16)
    sent_valid = jnp.sum(place, axis=(0, 1))
    got_docs, got_targs, got_valid = (
        lax.all_to_all(
            sent_docs.reshape(paths, micro, room, width),
            ("row", "col"),
            split_axis=0,
            concat_axis=0,
            tiled=True,
        ),
        lax.all_to_all(
            sent_targs.reshape(paths, micro, room, width),
            ("row", "col"),
            split_axis=0,
            concat_axis=0,
            tiled=True,
        ),
        lax.all_to_all(
            sent_valid.reshape(paths, micro, room),
            ("row", "col"),
            split_axis=0,
            concat_axis=0,
            tiled=True,
        ),
    )
    start_one = lax.all_gather(module_one.astype(jnp.bfloat16), "col", axis=1, tiled=True)[0]
    start_two = lax.all_gather(module_two.astype(jnp.bfloat16), "row", axis=1, tiled=True)[0]
    p_one = start_one.astype(jnp.float32)
    p_two = start_two.astype(jnp.float32)
    m_one = jnp.zeros_like(p_one)
    v_one = jnp.zeros_like(p_one)
    m_two = jnp.zeros_like(p_two)
    v_two = jnp.zeros_like(p_two)
    for step in range(micro):
        rows = got_docs[:, step].reshape(paths * room, width)
        targs = got_targs[:, step].reshape(paths * room, width)
        valid = got_valid[:, step].reshape(paths * room, 1).astype(jnp.float32)
        grad_one, grad_two = gradients(
            p_one.astype(jnp.bfloat16), p_two.astype(jnp.bfloat16), rows, targs, valid, rows_dev
        )
        p_one, m_one, v_one = adamw(p_one, grad_one, m_one, v_one, step, guard)
        p_two, m_two, v_two = adamw(p_two, grad_two, m_two, v_two, step, guard)
    delta_one = start_one.astype(jnp.float32) - p_one
    delta_two = start_two.astype(jnp.float32) - p_two
    counts = doc_counts.astype(jnp.float32)
    row_counts = lax.dynamic_index_in_dim(counts, row_id, 0, keepdims=False)
    col_counts = lax.dynamic_index_in_dim(counts, col_id, 1, keepdims=False)
    own_count = lax.dynamic_index_in_dim(row_counts, col_id, 0, keepdims=False)
    term_one = rounded(own_count / jnp.sum(row_counts) * delta_one)
    term_two = rounded(own_count / jnp.sum(col_counts) * delta_two)
    avg_one = lax.psum_scatter(
        term_one.astype(jnp.bfloat16), "col", scatter_dimension=0, tiled=True
    ).astype(jnp.float32)
    avg_two = lax.psum_scatter(
        term_two.astype(jnp.bfloat16), "row", scatter_dimension=0, tiled=True
    ).astype(jnp.float32)
    next_moment_one = outer_moment * moment_one + avg_one[None]
    next_moment_two = outer_moment * moment_two + avg_two[None]
    new_one = module_one - outer_rate * (outer_moment * next_moment_one + avg_one[None])
    new_two = module_two - outer_rate * (outer_moment * next_moment_two + avg_two[None])
    return (new_one, new_two, next_moment_one, next_moment_two)


def solution(mesh):
    return jax.shard_map(
        shards,
        mesh=mesh,
        in_specs=(
            P(None, ("row", "col"), None),
            P(None, ("row", "col"), None),
            P(None, ("row", "col"), None),
            P(),
            P("row", "col", None),
            P("col", "row", None),
            P("row", "col", None),
            P("col", "row", None),
        ),
        out_specs=(
            P("row", "col", None),
            P("col", "row", None),
            P("row", "col", None),
            P("col", "row", None),
        ),
        check_vma=False,
    )
```

profile of v0, /device:TPU:1, one launch (start us, length us, event | category | flops | bytes accessed | tf_op | source)
XLA Modules:
  0.0 638.7 jit_solution(16033839369389731655)
XLA Ops:
  7.2 0.0 copy-start
  7.2 0.0 copy-start.3
  7.2 0.0 copy-start.7
  7.2 0.0 all-gather.3.cloned.1.call-start
  7.2 4.0 convert_element_type.110
  11.2 0.0 all-gather.3.cloned.1.call-update
  11.3 0.0 all-gather.5.cloned.1.call-start
  11.3 0.0 copy-done.3
  11.3 1.1 convert_element_type.116
  12.4 0.0 all-gather.5.cloned.1.call-update
  12.5 0.0 copy-done.7
  12.5 0.1 fusion.67
  12.6 0.2 reduce_window_sum.11
  12.8 0.2 select_reduce_fusion
  12.9 0.1 add_add_fusion
  13.0 0.2 fusion.64
  13.2 0.7 reshape.55
  13.9 7.1 %all-to-all-start.2 = ((bf16[32,2,8]{2,1,0:T(2,128)(2,1)}), bf16[32,2,8]{2,1,0:T(2,128)(2,1)S(1)}, u32[]{:S(2)}, u32[]{:S(2)}) async-start(bf16[32,2,8]{2,1,0:T(2,128)(2,1)} %reshape.55), calls=%async_computation.2 | async-start | bytes 32768 | tf_op jit(solution)/shard_map/all_to_all | solution.py:101
  21.0 0.0 copy-done
  21.0 2.0 bitcast_convert_fusion.1
  23.0 4.6 all-to-all-done.2
  27.6 3.1 all-to-all-start
  30.7 3.3 bitcast_convert_fusion
  34.0 94.3 %all-to-all-done = bf16[32,2,8,2048]{3,2,1,0:T(8,128)(2,1)S(1)} async-done(((bf16[32,2,8,2048]{3,2,1,0:T(8,128)(2,1)}), bf16[32,2,8,2048]{3,2,1,0:T(8,128)(2,1)S(1)}, u32[]{:S(2)}, u32[]{:S(2)}) %all-to-all-start) | async-done | bytes 2097184 | tf_op jit(solution)/shard_map/all_to_all | solution.py:87
  128.3 10.4 %all-to-all-start.1 = ((bf16[32,2,8,2048]{3,2,1,0:T(8,128)(2,1)}), bf16[32,2,8,2048]{3,2,1,0:T(8,128)(2,1)}, u32[]{:S(2)}, u32[]{:S(2)}) async-start(bf16[32,2,8,2048]{3,2,1,0:T(8,128)(2,1)} %bitcast.10), calls=%async_computation.1 | async-start | bytes 4194304 | tf_op jit(solution)/shard_map/all_to_all | solution.py:94
  138.7 0.0 reduce-scatter.5.cloned.1.call-start
  138.7 0.0 copy-done.8
  138.8 0.0 copy-start.5
  138.8 0.6 dynamic-slice_reduce_fusion.1
  139.4 0.6 dynamic_slice.12
  140.0 0.0 copy-done.5
  141.2 0.1 fusion.68
  141.3 0.1 reshape.59
  141.4 0.1 reshape.57
  141.5 111.2 %all-gather.3.cloned.1.call-done = bf16[1,2048,2048]{2,1,0:T(8,128)(2,1)} async-done(((bf16[1,512,2048]{2,1,0:T(8,128)(2,1)}), bf16[1,2048,2048]{2,1,0:T(8,128)(2,1)}) %all-gather.3.cloned.1.call-update) | async-done | bytes 8388624 | tf_op jit(solution)/shard_map/all_gather | solution.py:109
  252.7 7.1 %fusion.19 = f32[256,2048]{1,0:T(8,128)} fusion(bf16[1,2048,2048]{2,1,0:T(8,128)(2,1)} %all-gather.3.cloned.1.call-done, bf16[32,2,8,2048]{3,2,1,0:T(8,128)(2,1)S(1)} %all-to-all-done), kind=kOutput, calls=%fused_computation.31 | convolution fusion | flops 2148007936 | bytes 11534336 | tf_op jit(solution)/shard_map/dot_general | solution.py:24
  259.8 0.0 all-to-all-done.1
  259.8 48.2 %all-gather.5.cloned.1.call-done = bf16[1,2048,2048]{2,1,0:T(8,128)(2,1)} async-done(((bf16[1,256,2048]{2,1,0:T(8,128)(2,1)}), bf16[1,2048,2048]{2,1,0:T(8,128)(2,1)}) %all-gather.5.cloned.1.call-update) | async-done | bytes 8388624 | tf_op jit(solution)/shard_map/all_gather | solution.py:110
  308.0 7.0 %fusion.51 = bf16[256,2048]{1,0:T(8,128)(2,1)S(1)} fusion(bf16[1,2048,2048]{2,1,0:T(8,128)(2,1)} %all-gather.5.cloned.1.call-done, bf16[32,2,8,2048]{3,2,1,0:T(8,128)(2,1)} %all-to-all-done.1, f32[256]{0:T(256)S(1)} %reshape.57, bf16[32,2,8,2048]{3,2,1,0:T(8,128)(2,1)S(1)} %all-to-all-done, f32[256,2048]{1,0:T(8,128)} %fusion.19), kind=kOutput, calls=%fused_computation.49 | convolution fusion | flops 2154299392 | bytes 13632512 | tf_op jit(solution)/shard_map/dot_general | solution.py:28
  315.0 0.0 copy-done.9
  315.0 0.2 copy-done.10
  315.2 2.8 fusion.56
  318.1 15.9 %fusion.16 = (bf16[2048,2048]{1,0:T(8,128)(2,1)}, f32[2048,2048]{1,0:T(8,128)}) fusion(bf16[1,2048,2048]{2,1,0:T(8,128)(2,1)S(1)} %copy-done.9, bf16[256,2048]{1,0:T(8,128)(2,1)S(1)} %fusion.51, f32[256,2048]{1,0:T(8,128)S(1)} %copy-done.10), kind=kOutput, calls=%fused_computation.26 | convolution fusion | flops 2204631040 | bytes 36700160 | tf_op jit(solution)/shard_map/dot_general | solution.py:32
  334.0 2.4 fusion.61
  336.3 0.0 copy-start.2
  336.3 29.0 %fusion.32 = f32[256,2048]{1,0:T(8,128)S(1)} fusion(f32[2048,2048]{1,0:T(8,128)S(1)} %fusion.61, bf16[1,2048,2048]{2,1,0:T(8,128)(2,1)} %all-gather.3.cloned.1.call-done, bf16[32,2,8,2048]{3,2,1,0:T(8,128)(2,1)S(1)} %all-to-all-done), kind=kOutput, calls=%fused_computation.38 | convolution fusion | flops 2202533888 | bytes 28311552 | tf_op jit(solution)/shard_map/dot_general | solution.py:24
  365.3 0.0 copy-done.2
  365.4 0.0 copy-start.11
  365.4 0.0 copy-start.13
  365.4 7.1 %fusion.54 = bf16[256,2048]{1,0:T(8,128)(2,1)S(1)} fusion(bf16[2048,2048]{1,0:T(8,128)(2,1)} %get-tuple-element.10, bf16[32,2,8,2048]{3,2,1,0:T(8,128)(2,1)} %all-to-all-done.1, f32[256]{0:T(256)S(1)} %reshape.59, bf16[32,2,8,2048]{3,2,1,0:T(8,128)(2,1)S(1)} %all-to-all-done, f32[256,2048]{1,0:T(8,128)S(1)} %fusion.32), kind=kOutput, calls=%fused_computation.50 | convolution fusion | flops 2154299392 | bytes 13632512 | tf_op jit(solution)/shard_map/dot_general | solution.py:28
  372.5 0.0 copy-start.12
  372.5 1.0 copy-done.12
  373.5 1.5 copy-done.13
  375.0 29.9 %fusion.7 = bf16[2048,2048]{1,0:T(8,128)(2,1)} fusion(f32[2048,2048]{1,0:T(8,128)S(1)} %copy-done.13, bf16[1,2048,2048]{2,1,0:T(8,128)(2,1)} %all-gather.5.cloned.1.call-done, f32[]{:T(128)S(6)} %div.74, bf16[256,2048]{1,0:T(8,128)(2,1)S(1)} %fusion.54, f32[256,2048]{1,0:T(8,128)S(1)} %fusion.32), kind=kOutput, calls=%fused_computation.13 | convolution fusion | flops 2280128512 | bytes 36700164 | tf_op jit(solution)/shard_map/dot_general | solution.py:32
  404.8 0.0 reduce-scatter.5.cloned.1.call-update
  404.9 0.0 reduce-scatter.3.cloned.1.call-start
  404.9 0.6 copy-done.6
  405.5 0.7 dynamic-slice_reduce_fusion
  407.4 35.7 %fusion.3 = bf16[2048,2048]{1,0:T(8,128)(2,1)} fusion(f32[2048,2048]{1,0:T(8,128)} %copy-done.2, bf16[1,2048,2048]{2,1,0:T(8,128)(2,1)} %all-gather.3.cloned.1.call-done, f32[]{:T(128)S(6)} %div.59, bf16[32,2,8,2048]{3,2,1,0:T(8,128)(2,1)S(1)} %all-to-all-done, bf16[256,2048]{1,0:T(8,128)(2,1)} %copy-done.12, bf16[2048,2048]{1,0:T(8,128)(2,1)} %get-tuple-element.10, ...), kind=kOutput, calls=%fused_computation.9 | convolution fusion | flops 4430233600 | bytes 46137348 | tf_op jit(solution)/shard_map/dot_general | solution.py:41
  443.2 0.0 reduce-scatter.3.cloned.1.call-update
  443.2 32.6 %reduce-scatter.5.cloned.1.call-done = bf16[256,2048]{1,0:T(8,128)(2,1)} async-done(((bf16[2048,2048]{1,0:T(8,128)(2,1)}), bf16[256,2048]{1,0:T(8,128)(2,1)}) %reduce-scatter.5.cloned.1.call-update) | async-done | bytes 1048592 | tf_op jit(solution)/shard_map/reduce_scatter | solution.py:137
  475.8 4.7 fusion.60
  480.5 141.9 %reduce-scatter.3.cloned.1.call-done = bf16[512,2048]{1,0:T(8,128)(2,1)} async-done(((bf16[2048,2048]{1,0:T(8,128)(2,1)}), bf16[512,2048]{1,0:T(8,128)(2,1)}) %reduce-scatter.3.cloned.1.call-update) | async-done | bytes 2097168 | tf_op jit(solution)/shard_map/reduce_scatter | solution.py:134
  622.5 9.5 %fusion.18 = (f32[1,512,2048]{2,1,0:T(8,128)}, f32[1,512,2048]{2,1,0:T(8,128)}) fusion(f32[1,512,2048]{2,1,0:T(8,128)} %param.12, bf16[512,2048]{1,0:T(8,128)(2,1)} %reduce-scatter.3.cloned.1.call-done, f32[1,512,2048]{2,1,0:T(8,128)} %param.14), kind=kLoop, calls=%fused_computation.28 | loop fusion | flops 7340032 | bytes 18874368 | tf_op jit(solution)/shard_map/sub | solution.py:142
  (11 shorter events, 0.0 us)
Async XLA Ops:
  7.2 13.8 %copy-start = (bf16[2,128,2048]{2,1,0:T(8,128)(2,1)S(1)}, bf16[2,128,2048]{2,1,0:T(8,128)(2,1)}, u32[]{:S(2)}) copy-start(bf16[2,128,2048]{2,1,0:T(8,128)(2,1)} %param.8) | copy-start | bytes 3145732
  7.2 4.1 copy-start.3
  7.2 5.3 copy-start.7
  7.2 245.5 %all-gather.3.cloned.1.call-start = ((), (), s32[]{:S(2)}) async-start(), calls=%async_computation.5 | async-start | bytes 10485760 | tf_op jit(solution)/shard_map/all_gather | solution.py:109
  11.3 296.7 %all-gather.5.cloned.1.call-start = ((), (), s32[]{:S(2)}) async-start(), calls=%async_computation.6 | async-start | bytes 9437184 | tf_op jit(solution)/shard_map/all_gather | solution.py:110
  12.4 126.3 %copy-start.8 = (s32[8,4]{0,1:T(4,128)S(1)}, s32[8,4]{0,1:T(4,128)}, u32[]{:S(2)}) copy-start(s32[8,4]{0,1:T(4,128)} %param.11) | copy-start | bytes 388
  13.9 13.7 %all-to-all-start.2 = ((bf16[32,2,8]{2,1,0:T(2,128)(2,1)}), bf16[32,2,8]{2,1,0:T(2,128)(2,1)S(1)}, u32[]{:S(2)}, u32[]{:S(2)}) async-start(bf16[32,2,8]{2,1,0:T(2,128)(2,1)} %reshape.55), calls=%async_computation.2 | async-start | bytes 32768 | tf_op jit(solution)/shard_map/all_to_all | solution.py:101
  27.6 100.6 %all-to-all-start = ((bf16[32,2,8,2048]{3,2,1,0:T(8,128)(2,1)}), bf16[32,2,8,2048]{3,2,1,0:T(8,128)(2,1)S(1)}, u32[]{:S(2)}, u32[]{:S(2)}) async-start(bf16[32,2,8,2048]{3,2,1,0:T(8,128)(2,1)} %bitcast.6), calls=%async_computation | async-start | bytes 4194304 | tf_op jit(solution)/shard_map/all_to_all | solution.py:87
  128.3 131.5 %all-to-all-start.1 = ((bf16[32,2,8,2048]{3,2,1,0:T(8,128)(2,1)}), bf16[32,2,8,2048]{3,2,1,0:T(8,128)(2,1)}, u32[]{:S(2)}, u32[]{:S(2)}) async-start(bf16[32,2,8,2048]{3,2,1,0:T(8,128)(2,1)} %bitcast.10), calls=%async_computation.1 | async-start | bytes 4194304 | tf_op jit(solution)/shard_map/all_to_all | solution.py:94
  138.7 337.1 %reduce-scatter.5.cloned.1.call-start = ((), (), s32[]{:S(2)}) async-start(), calls=%async_computation.8 | async-start | bytes 9437184 | tf_op jit(solution)/shard_map/reduce_scatter | solution.py:137
  138.8 1.2 copy-start.5
  308.0 7.0 %copy-start.9 = (bf16[1,2048,2048]{2,1,0:T(8,128)(2,1)S(1)}, bf16[1,2048,2048]{2,1,0:T(8,128)(2,1)}, u32[]{:S(2)}) copy-start(bf16[1,2048,2048]{2,1,0:T(8,128)(2,1)} %all-gather.5.cloned.1.call-done) | copy-start | bytes 25165828
  308.0 7.3 %copy-start.10 = (f32[256,2048]{1,0:T(8,128)S(1)}, f32[256,2048]{1,0:T(8,128)}, u32[]{:S(2)}) copy-start(f32[256,2048]{1,0:T(8,128)} %fusion.19) | copy-start | bytes 6291460
  336.3 29.0 %copy-start.2 = (f32[2048,2048]{1,0:T(8,128)}, f32[2048,2048]{1,0:T(8,128)S(1)}, u32[]{:S(2)}) copy-start(f32[2048,2048]{1,0:T(8,128)S(1)} %fusion.61) | copy-start | bytes 50331652
  365.4 7.2 %copy-start.11 = (f32[256,2048]{1,0:T(8,128)}, f32[256,2048]{1,0:T(8,128)S(1)}, u32[]{:S(2)}) copy-start(f32[256,2048]{1,0:T(8,128)S(1)} %fusion.32) | copy-start | bytes 6291460
  365.4 9.6 %copy-start.13 = (f32[2048,2048]{1,0:T(8,128)S(1)}, f32[2048,2048]{1,0:T(8,128)}, u32[]{:S(2)}) copy-start(f32[2048,2048]{1,0:T(8,128)} %get-tuple-element.11) | copy-start | bytes 50331652
  372.5 1.0 copy-start.12
  404.8 0.7 copy-start.6
  404.9 217.6 %reduce-scatter.3.cloned.1.call-start = ((), (), s32[]{:S(2)}) async-start(), calls=%async_computation.7 | async-start | bytes 10485760 | tf_op jit(solution)/shard_map/reduce_scatter | solution.py:134
  443.2 32.7 %copy-start.4 = (f32[1,256,2048]{2,1,0:T(8,128)S(1)}, f32[1,256,2048]{2,1,0:T(8,128)}, u32[]{:S(2)}) copy-start(f32[1,256,2048]{2,1,0:T(8,128)} %param.13) | copy-start | bytes 6291460
  475.8 156.1 %copy-start.1 = (bf16[2,128,2048]{2,1,0:T(8,128)(2,1)S(1)}, bf16[2,128,2048]{2,1,0:T(8,128)(2,1)}, u32[]{:S(2)}) copy-start(bf16[2,128,2048]{2,1,0:T(8,128)(2,1)} %param.8) | copy-start | bytes 3145732
Sparse Core Ops, SparseCore 0:
  11.4 241.3 all-gather.2
  255.2 52.7 all-gather.4
  405.0 70.7 reduce-scatter.4
  478.1 144.2 reduce-scatter.2
where the time goes:
time: 642 us; the launch traced here: 639 us
  waiting for transfers between devices  433 us (67%)
  matrix products  142 us (22%)
  other arithmetic  21.4 us (3%)
  starting transfers between devices  20.8 us (3%)
  between operations  16.7 us (3%)
    reduce_scatter x1, waiting for transfers between devices, shards(): lax.psum_scatter(term_one.astype(jnp.bfloat16), 'col', scatter_dimension=...  142 us
    all_gather x1, waiting for transfers between devices, shards(): lax.all_gather(module_one.astype(jnp.bfloat16), 'col', axis=1, tiled=True)  111 us
    all_to_all x1, waiting for transfers between devices, shards(): lax.all_to_all(sent_docs.reshape(paths, micro, room, width), ('row', 'col...  94.3 us
    all_gather x1, waiting for transfers between devices, shards(): lax.all_gather(module_two.astype(jnp.bfloat16), 'row', axis=1, tiled=True)  48.2 us
    dot_general x2, matrix products, gradients(): lax.dot_general(hidden, error, (((0,), (0,)), ((), ())), preferred_elemen...  45.8 us
    dot_general x2, matrix products, gradients(): lax.dot_general(rows, inner, (((0,), (0,)), ((), ())), preferred_element_...  38.1 us
    dot_general x2, matrix products, gradients(): pre = jnp.dot(rows, w_one, preferred_element_type=jnp.float32) * scale  36 us
    reduce_scatter x1, waiting for transfers between devices, shards(): lax.psum_scatter(term_two.astype(jnp.bfloat16), 'row', scatter_dimension=...  32.6 us
  transfers between devices with their start and end apart: 7, of which 6 were waited for; matrix products, arithmetic and copies ran while one was open for 9% of the time, Pallas kernels for 0%

commit v1 on v0

v1 whole, which is shorter than its diff:
```python
import functools

import jax
import jax.numpy as jnp
from jax import lax
from jax.experimental import pallas as pl
from jax.experimental.pallas import tpu as pltpu
from jax.sharding import PartitionSpec as P

beta_one = 0.9
beta_two = 0.95
inner_rate = 0.1
decay = 0.1
outer_rate = 0.7
outer_moment = 0.9

VMEM_LIMIT = 56 * 1024 * 1024
f32 = jnp.float32
bf16 = jnp.bfloat16


def step_kernel(rows_dev, tile, keep, base, one_at, two_at, *refs):
    n_one, n_two = len(one_at), len(two_at)
    place_ref, xy_ref = refs[:2]
    refs = refs[2:]

    def take(places):
        nonlocal refs
        found = [tuple(refs[sum(p[1] for p in places[:i]) :][: p[1]]) for i, p in enumerate(places)]
        refs = refs[sum(p[1] for p in places) :]
        return found

    one_refs, two_refs = take(one_at), take(two_at)
    left_ref, right_ref = refs[:2]
    start_out = refs[2] if keep else None
    one, two, pre, one_sem, two_sem, out_sem = refs[-6:]
    width = one.shape[0]
    scale = width ** (-0.5)
    parts = width // tile
    home = place_ref[base + n_one + n_two]

    class Copies:
        def __init__(self, *choices):
            self.choices = choices

        def start(self):
            if len(self.choices) == 1:
                self.choices[0].start()
            else:
                pl.when(home == 1)(self.choices[0].start)
                pl.when(home == 0)(self.choices[1].start)

        def wait(self):
            self.choices[0].wait()

    def one_copies(n):
        found = []
        for i, (pieces, (first, _, top, tall)) in enumerate(zip(one_refs, one_at)):
            wide = pieces[0].shape[1]
            if first <= n * tile < first + wide:
                down = pl.ds(pl.multiple_of(place_ref[base + i] * tall, tall), tall)
                found.append(
                    Copies(*[
                        pltpu.make_async_copy(
                            piece.at[pl.ds(top, tall), pl.ds(n * tile - first, tile)],
                            one.at[down, pl.ds(n * tile, tile)],
                            one_sem.at[i, n],
                        )
                        for piece in pieces
                    ])
                )
        return found

    two_copies = []
    for i, (pieces, (first, _, top, tall)) in enumerate(zip(two_refs, two_at)):
        wide = pieces[0].shape[1]
        down = pl.ds(pl.multiple_of(place_ref[base + n_one + i] * tall, tall), tall)
        two_copies.append(
            Copies(*[
                pltpu.make_async_copy(piece.at[pl.ds(top, tall), :], two.at[down, pl.ds(first, wide)], two_sem.at[i])
                for piece in pieces
            ])
        )
    for n in range(parts):
        for copy in one_copies(n):
            copy.start()
    for copy in two_copies:
        copy.start()
    for n in range(parts):
        span = pl.ds(n * tile, tile)
        for copy in one_copies(n):
            copy.wait()
        value = jnp.dot(xy_ref[:, :width], one[:, span], preferred_element_type=f32) * scale
        pre[:, span] = value
        left_ref[:, span] = xy_ref[:, span]
        left_ref[:, pl.ds(width + n * tile, tile)] = (value * jax.nn.sigmoid(value)).astype(bf16)
    for copy in two_copies:
        copy.wait()
    if keep:
        one_save = pltpu.make_async_copy(one, start_out.at[pl.ds(0, width), :], out_sem.at[0])
        two_save = pltpu.make_async_copy(two, start_out.at[pl.ds(width, width), :], out_sem.at[1])
        one_save.start()
        two_save.start()

    def miss(n, carry):
        span = pl.ds(pl.multiple_of(n * tile, tile), tile)
        late = pl.ds(pl.multiple_of(width + n * tile, tile), tile)
        out = xy_ref[:, span].astype(f32) + jnp.dot(left_ref[:, width:], two[:, span], preferred_element_type=f32) * scale
        right_ref[:, late] = ((out - xy_ref[:, late].astype(f32)) / rows_dev).astype(bf16)
        return carry

    lax.fori_loop(0, parts, miss, 0)

    def backward(n, carry):
        span = pl.ds(pl.multiple_of(n * tile, tile), tile)
        back = lax.dot_general(
            right_ref[:, width:], two[span, :], (((1,), (1,)), ((), ())), preferred_element_type=f32
        ) * scale
        value = pre[:, span]
        sig = jax.nn.sigmoid(value)
        right_ref[:, span] = (back * (sig * (1.0 + value * (1.0 - sig)))).astype(bf16)
        return carry

    lax.fori_loop(0, parts, backward, 0)
    if keep:
        one_save.wait()
        two_save.wait()


def step(xy, one, two, rows_dev, keep, places, base):
    rows, width = xy.shape[0], xy.shape[1] // 2
    tile = 512
    vmem = pl.BlockSpec(memory_space=pltpu.VMEM)
    hbm = pl.BlockSpec(memory_space=pl.ANY)
    out = jax.ShapeDtypeStruct((rows, 2 * width), bf16)
    whole = jax.ShapeDtypeStruct((2 * width, width), bf16)
    sources = [array for p in one + two for array in p[0]]

    def entries(pieces):
        return tuple((p[1], len(p[0]), *(p[2:] or (0, p[0][0].shape[0]))) for p in pieces)

    return pl.pallas_call(
        functools.partial(
            step_kernel, rows_dev, tile, keep, base, entries(one), entries(two)
        ),
        out_shape=(out, out) + ((whole,) if keep else ()),
        in_specs=[pl.BlockSpec(memory_space=pltpu.SMEM), vmem] + [hbm] * len(sources),
        out_specs=(vmem, vmem) + ((hbm,) if keep else ()),
        scratch_shapes=[
            pltpu.VMEM((width, width), bf16),
            pltpu.VMEM((width, width), bf16),
            pltpu.VMEM((rows, width), f32),
            pltpu.SemaphoreType.DMA((len(one), width // tile)),
            pltpu.SemaphoreType.DMA((len(two),)),
            pltpu.SemaphoreType.DMA((2,)),
        ],
        compiler_params=pltpu.CompilerParams(vmem_limit_bytes=VMEM_LIMIT),
        cost_estimate=pl.CostEstimate(flops=15 * rows * width * width, bytes_accessed=4 * width * width, transcendentals=0),
    )(places, xy, *sources)


def update_kernel(guard, tile, a_ref, b_ref, p_ref, out_ref):
    shrink = inner_rate * decay
    turned = a_ref[...].T
    for n in range(p_ref.shape[1] // tile):
        span = slice(n * tile, (n + 1) * tile)
        grad = jnp.dot(turned, b_ref[:, span], preferred_element_type=f32)
        move = grad * pl.reciprocal(jnp.abs(grad) + guard, approx=True)
        out_ref[:, span] = (p_ref[:, span].astype(f32) * (1.0 - shrink) - inner_rate * move).astype(bf16)


def update(left, right, start, guard):
    rows, width = left.shape[0], start.shape[1]
    tall = 512
    each = width // tall
    return pl.pallas_call(
        functools.partial(update_kernel, guard * width ** 0.5, 512),
        out_shape=jax.ShapeDtypeStruct(start.shape, bf16),
        grid=(2 * each,),
        in_specs=[
            pl.BlockSpec((rows, tall), lambda m: (0, m)),
            pl.BlockSpec((rows, width), lambda m: (0, m // each)),
            pl.BlockSpec((tall, width), lambda m: (m, 0)),
        ],
        out_specs=pl.BlockSpec((tall, width), lambda m: (m, 0)),
        compiler_params=pltpu.CompilerParams(vmem_limit_bytes=VMEM_LIMIT),
        cost_estimate=pl.CostEstimate(flops=12 * rows * width * start.shape[0], bytes_accessed=4 * start.size, transcendentals=0),
    )(left, right, start)


def term_kernel(guard, tile, base, spans, place_ref, weight_ref, a_ref, b_ref, c_ref, d_ref, p_ref, *refs):
    outs, held, sem = refs[:-2], refs[-2], refs[-1]
    step = pl.program_id(0)
    slot = step % 2
    last = spans[-1][1]
    short, wide = p_ref.shape

    def copies(m, slot):
        return [
            (
                (m >= begin) & (m < end),
                pltpu.make_async_copy(
                    held.at[slot], out.at[pl.ds(pl.multiple_of((m - begin) * short, short), short), :], sem.at[slot]
                ),
            )
            for out, (begin, end) in zip(outs, spans)
        ]

    def settle(slot):
        pltpu.make_async_copy(held.at[slot], outs[0].at[pl.ds(0, short), :], sem.at[slot]).wait()

    @pl.when(step >= 2)
    def _():
        settle(slot)

    weight = jnp.where(place_ref[base + 3 * last + step] == 0, weight_ref[0], weight_ref[1])
    shrink = inner_rate * decay
    new_m = (1.0 - beta_one) / (1.0 - beta_one ** 2)
    new_v = ((1.0 - beta_two) / (1.0 - beta_two ** 2)) ** 0.5
    by_first = weight * (inner_rate * (1.0 - shrink))
    by_second = weight * (inner_rate * new_m / new_v)
    by_start = weight * (shrink * (2.0 - shrink))
    older, newer = a_ref[...].T, c_ref[...].T
    for n in range(wide // tile):
        span = slice(n * tile, (n + 1) * tile)
        old = jnp.dot(older, b_ref[:, span], preferred_element_type=f32)
        new = jnp.dot(newer, d_ref[:, span], preferred_element_type=f32)
        first = old * pl.reciprocal(jnp.abs(old) + guard, approx=True)
        square = beta_two * (old * old) + new * new
        root = square * lax.rsqrt(square + 1e-30)
        second = (beta_one * old + new) * pl.reciprocal(root + guard / new_v, approx=True)
        start = p_ref[:, span].astype(f32)
        held[slot, :, span] = (first * by_first + second * by_second + start * by_start).astype(bf16)
    for here, copy in copies(step, slot):
        pl.when(here)(copy.start)

    @pl.when(step == last - 1)
    def _():
        settle(slot)
        if last > 1:
            settle(1 - slot)


def terms(weights, places, base, counts, short, parts, a, b, c, d, p, guard):
    rows, width = a.shape[0], p.shape[1]
    wide = width // parts
    ends = [sum(counts[: n + 1]) for n in range(len(counts))]
    spans = tuple((end - count, end) for count, end in zip(counts, ends))
    last = ends[-1]
    row = lambda m, at: at[base + m]
    col = lambda m, at: at[base + last + m]
    both = lambda m, at: at[base + 2 * last + m]
    side = pl.BlockSpec((rows, short), lambda m, at: (0, row(m, at)))
    full = pl.BlockSpec((rows, wide), lambda m, at: (0, both(m, at)))
    return pl.pallas_call(
        functools.partial(term_kernel, guard * width ** 0.5, 256, base, spans),
        out_shape=tuple(jax.ShapeDtypeStruct((count * short, wide), bf16) for count in counts),
        grid_spec=pltpu.PrefetchScalarGridSpec(
            num_scalar_prefetch=1,
            grid=(last,),
            in_specs=[
                pl.BlockSpec(memory_space=pltpu.SMEM),
                side, full, side, full,
                pl.BlockSpec((short, wide), lambda m, at: (row(m, at), col(m, at))),
            ],
            out_specs=tuple(pl.BlockSpec(memory_space=pl.ANY) for _ in counts),
            scratch_shapes=[pltpu.VMEM((2, short, wide), bf16), pltpu.SemaphoreType.DMA((2,))],
        ),
        compiler_params=pltpu.CompilerParams(vmem_limit_bytes=VMEM_LIMIT),
        cost_estimate=pl.CostEstimate(flops=1, bytes_accessed=1, transcendentals=0),
    )(places, weights, a, b, c, d, p)


def slots(routes, documents, targets, device_of, room):
    dest = device_of(routes[:, 0])
    paths = device_of(None)
    hit = (dest[:, None] == jnp.arange(paths, dtype=jnp.int32)[None, :]).astype(jnp.int32)
    before = jnp.cumsum(hit, axis=0) - hit
    slot = dest * room + jnp.sum(before * hit, axis=1)
    place = (slot[:, None] == jnp.arange(paths * room, dtype=jnp.int32)[None, :]).astype(bf16)
    both = jnp.concatenate([documents, targets], axis=1)
    return jnp.einsum("rs,rd->sd", place, both, preferred_element_type=f32).astype(bf16)


def after(value, *others):
    return lax.optimization_barrier((value,) + others)[0]


def shards(documents, targets, routes, doc_counts, module_one, module_two, moment_one, moment_two):
    n_row = lax.axis_size("row")
    n_col = lax.axis_size("col")
    chips, half = n_row // 2, n_col // 2
    paths = n_row * n_col
    row_id = lax.axis_index("row")
    col_id = lax.axis_index("col")
    chip, core = row_id // 2, row_id % 2
    side, turn = col_id // half, col_id % half
    home = core == side
    micro, rows_dev, width = documents.shape
    room = max(2, 2 * rows_dev // paths)
    guard = 0.5 / (width * rows_dev) ** 0.5

    def device_of(path):
        if path is None:
            return paths
        i, j = path // n_col, path % n_col
        return (2 * (i // 2) + j // half) * n_col + (i % 2) * half + j % half

    def send(value, target):
        pairs = []
        for i in range(n_row):
            for k in range(n_col):
                to = target(i // 2, i % 2, k // half, k % half)
                if to is not None:
                    c, b, h, q = to
                    pairs.append((i * n_col + k, (2 * c + b) * n_col + h * half + q))
        return lax.ppermute(value, ("row", "col"), pairs)

    def to_core(value):
        return send(value, lambda c, b, h, q: (c, 1 - b, h, q))

    def to_turn(value, s):
        return send(value, lambda c, b, h, q: (c, b, h, (q + s) % half))

    def to_chip(value, bit):
        return send(value, lambda c, b, h, q: (c ^ bit, b, h, q))

    bits = [1 << t for t in range(chips.bit_length() - 1)]
    orders = [bits, bits[::-1]]
    cols = width // 2

    every = list(range(chips))
    tall_one, tall_two = width // n_col, width // chips
    short = min(tall_one, tall_two, 512)
    table = []

    def enter(*pieces):
        talls = (tall_one, tall_two)
        listed = [
            (
                level * (width // short) + block * (talls[level] // short) + cut,
                part,
                level * 2 + part,
                level,
            )
            for level, blocks, part in pieces
            for block in blocks
            for cut in range(talls[level] // short)
        ]
        base = len(table)
        for field in zip(*listed):
            table.extend(field)
        return base, tuple(len(blocks) * (talls[level] // short) for level, blocks, part in pieces)

    here = [(turn + s) % half + core * half for s in range(half)]
    there = [(turn + s) % half + (1 - core) * half for s in range(half)]
    leave = [[chip ^ r for r in every if r & order[0]] for order in orders]
    stay = [[chip ^ r for r in every if not r & order[0]] for order in orders]
    calls = [
        enter((0, there, 0), (0, there, 1)),
        enter((0, here, 0), (0, here, 1)),
        enter((1, leave[0], 0), (1, leave[1], 1)),
        enter((1, stay[0], 0), (1, stay[1], 1)),
    ]
    base_first = len(table)
    for part in range(2):
        for s in range(half):
            table += [(turn - s) % half + core * half, (turn - s) % half + (1 - core) * half]
    table += [chip ^ r for part in range(2) for r in every] + [home]
    base_second = len(table)
    table += [0, 0, 0]
    places = jnp.stack([jnp.asarray(value).astype(jnp.int32) for value in table])

    counts = doc_counts.astype(f32)
    path_one, path_two = 2 * chip + side, turn + core * half
    in_row = (jnp.arange(n_row) == path_one)[:, None]
    in_col = (jnp.arange(n_col) == path_two)[None, :]
    row_counts = jnp.sum(jnp.where(in_row, counts, 0.0))
    col_counts = jnp.sum(jnp.where(in_col, counts, 0.0))
    own_count = jnp.sum(jnp.where(in_row & in_col, counts, 0.0))
    weights = jnp.stack([own_count / row_counts, own_count / col_counts])

    sent = [slots(routes[s], documents[s], targets[s], device_of, room) for s in range(micro)]

    def exchange(value):
        return lax.all_to_all(
            value.reshape(paths, room, 2 * width), ("row", "col"), split_axis=0, concat_axis=0, tiled=True
        ).reshape(paths * room, 2 * width)

    own_two = module_two[0].astype(bf16)
    own_one = module_one[0].astype(bf16)
    other_two = send(own_two, lambda c, b, h, q: (c, h, h, q) if b != h else None)
    pair_two = jnp.where(
        core == 0,
        jnp.concatenate([own_two, other_two], axis=0),
        jnp.concatenate([other_two, own_two], axis=0),
    )
    pair_two = [pair_two[:, :cols], pair_two[:, cols:]]

    def far_two(part, *others):
        return send(after(pair_two[part], *others), lambda c, b, h, q: (c, b, 1 - h, q) if b == h else None)

    def spread(held, bit, here):
        return held | {
            r ^ bit: send(value, lambda c, b, h, q: (c ^ bit, b, h, q) if (b == h) == here else None)
            for r, value in sorted(held.items())
        }

    def rest(held, here):
        for n in range(1, len(bits)):
            held = [spread(held[part], orders[part][n], here) for part in range(2)]
        return held

    def values(held):
        return [value for part in held for value in part.values()]

    ones = [own_one[:, :cols], own_one[:, cols:]]

    def shift(value, here):
        if half == 1:
            return jnp.zeros_like(value)
        return send(value, lambda c, b, h, q: (c, b, h, (q + 1) % half) if (b == h) == here else None)

    def far_one(part, *others):
        return send(
            after(ones[part], *others), lambda c, b, h, q: (c, 1 - b, 1 - h, q) if b != h else None
        )

    got_a = exchange(sent[0])
    shift_a = shift(ones[0], True)
    shift_b = shift(ones[1], True)
    home_two = [spread({0: pair_two[part]}, orders[part][0], True) for part in range(2)]
    home_two = rest(home_two, True)
    far_a = far_two(0)
    far_b = far_two(1)
    first = (got_a, shift_a, shift_b, far_a, far_b, *values(home_two))
    away_two = [spread({0: far}, orders[part][0], False) for part, far in enumerate((far_a, far_b))]
    one_a = far_one(0, *first)
    one_b = far_one(1, one_a, *values(away_two), places, weights, *sent[1:])
    turn_a = shift(one_a, False)
    away_two = rest(away_two, False)
    turn_b = shift(after(one_b, turn_a, *values(away_two)), False)
    one = []
    for part, (own, far, near, turned) in enumerate(
        ((ones[0], one_a, shift_a, turn_a), (ones[1], one_b, shift_b, turn_b))
    ):
        first = jnp.where(home, own, far)
        held = [first]
        if half > 1:
            held.append(jnp.where(home, near, turned))
        held += [to_turn(first, s) for s in range(2, half)]
        for value in held:
            one.append(((value,), part * cols))
            one.append(((to_core(value),), part * cols))
    two = [((home_two[part][r], away_two[part][r]), part * cols) for part in range(2) for r in every]
    got_b = exchange(after(sent[1], got_a, *[p[0][0] for p in one + two]))
    left_a, right_a, start = step(got_a, one, two, rows_dev, True, places, base_first)
    moved = update(left_a, right_a, start, guard)
    left_b, right_b = step(got_b, [((moved,), 0, 0, width)], [((moved,), 0, width, width)], rows_dev, False, places, base_second)

    def deltas(call, *others):
        return terms(after(weights, *others), places, *call, short, 2, left_a, right_a, left_b, right_b, start, guard)

    def summed(*values):
        return functools.reduce(lambda x, y: x + y, [value.astype(f32) for value in values])

    def both_cores(here, there):
        there = to_core(there)
        cuts = [slice(s * tall_one, (s + 1) * tall_one) for s in range(half)]
        return [(here[cut], there[cut]) for cut in cuts]

    def along(both, sums):
        return [*both[0], *[to_turn(value, s) for s, value in enumerate(sums, 1)]]

    def to_owner(terms):
        return send(summed(*terms).astype(bf16), lambda c, b, h, q: (c, 1 - b, 1 - h, q) if b != h else None)

    def chip_sum(part, here, there, *others):
        order = orders[part]
        there = to_chip(there, order[0])
        held = {}
        for n, r in enumerate(r for r in every if not r & order[0]):
            cut = slice(n * tall_two, (n + 1) * tall_two)
            held[r] = [here[cut], there[cut]]
        for bit in order[1:]:
            for r in [r for r in sorted(held) if r & bit]:
                held[r ^ bit].append(to_chip(after(summed(*held.pop(r)).astype(bf16), *others), bit))
        return held[0]

    def half_sum(parts, firsts, *others):
        fars = [
            send(
                after(summed(*terms).astype(bf16), first),
                lambda c, b, h, q: (c, b, 1 - h, q) if b != h else None,
            )
            for terms, first in zip(parts, firsts)
        ]
        sums = []
        for terms, far in zip(parts, fars):
            total = summed(*terms, far)
            up, down = total[: tall_two // 2], total[tall_two // 2 :]
            passed = send(
                after(jnp.where(core == 0, down, up).astype(bf16), *others),
                lambda c, b, h, q: (c, 1 - b, h, q) if b == h else None,
            )
            sums.append(jnp.where(home, jnp.where(core == 0, up, down), passed.astype(f32)))
        return sums

    def outer(module, moment, sums):
        average = jnp.concatenate(sums, axis=1)[None]
        following = outer_moment * moment + average
        return module - outer_rate * (outer_moment * following + average), following

    there_a, there_b = deltas(calls[0])
    here_a, here_b = deltas(calls[1], there_a)
    both_a, both_b = both_cores(here_a, there_a), both_cores(here_b, there_b)
    sums_a, sums_b = ([summed(*pair).astype(bf16) for pair in both[1:]] for both in (both_a, both_b))
    leave_a, leave_b = deltas(calls[2], here_a, *sums_a, *sums_b)
    along_a, along_b = along(both_a, sums_a), along(both_b, sums_b)
    stay_a, stay_b = deltas(calls[3], leave_a, along_a[-1])
    owned_a, owned_b = to_owner(along_a), to_owner(along_b)
    sums_one = [
        jnp.where(home, summed(*terms), owned.astype(f32))
        for terms, owned in ((along_a, owned_a), (along_b, owned_b))
    ]
    new_one, next_moment_one = outer(module_one, moment_one, sums_one)
    chip_a = chip_sum(0, stay_a, leave_a, owned_a)
    chip_b = chip_sum(1, stay_b, leave_b, owned_a)
    sums_two = half_sum((chip_a, chip_b), (owned_b, owned_b), new_one, next_moment_one)
    new_two, next_moment_two = outer(module_two, moment_two, sums_two)
    return (new_one, new_two, next_moment_one, next_moment_two)


def solution(mesh):
    return jax.shard_map(
        shards,
        mesh=mesh,
        in_specs=(
            P(None, ("row", "col"), None),
            P(None, ("row", "col"), None),
            P(None, ("row", "col"), None),
            P(),
            P("row", "col", None),
            P("col", "row", None),
            P("row", "col", None),
            P("col", "row", None),
        ),
        out_specs=(
            P("row", "col", None),
            P("col", "row", None),
            P("row", "col", None),
            P("col", "row", None),
        ),
        check_vma=False,
    )
```

time: 642 us -> 455 us (0.71)
  waiting for transfers between devices: 433 us -> 217 us
  matrix products: 142 us -> 4.28 us
  Pallas kernels: 0 us -> 94.3 us
  starting transfers between devices: 20.8 us -> 74.2 us
  other arithmetic: 21.4 us -> 49.2 us
  between operations: 16.7 us -> 4.29 us
    ppermute x0 -> x39, waiting for transfers between devices: none -> 204 us  [send(): return lax.ppermute(value, ('row', 'col'), pairs)]
    reduce_scatter x2 -> x0, waiting for transfers between devices: 175 us -> none  [the longest x1 142 us: shards(): lax.psum_scatter(term_one.astype(jnp.bfloat16), 'col', scatter_dimension=...]
    all_gather x2 -> x0, waiting for transfers between devices: 159 us -> none  [the longest x1 111 us: shards(): lax.all_gather(module_one.astype(jnp.bfloat16), 'col', axis=1, tiled=True)]
    dot_general x11 -> x2, matrix products: 142 us -> 4.28 us  [slots(): jnp.einsum('rs,rd->sd', place, both, preferred_element_type=f32)]
    pallas_call x0 -> x7, Pallas kernels: none -> 94.3 us  [the longest x4 43.8 us: terms(): pl.pallas_call(functools.partial(term_kernel, guard * width ** 0.5, 256,...]
    all_to_all x3 -> x2, waiting for transfers between devices: 98.9 us -> 12.9 us  [exchange(): lax.all_to_all(value.reshape(paths, room, 2 * width), ('row', 'col'), spl...]
    ppermute x0 -> x39, starting transfers between devices: none -> 62.2 us  [send(): return lax.ppermute(value, ('row', 'col'), pairs)]
    convert_element_type x5 -> x14, other arithmetic: 5.29 us -> 22.5 us  [the longest x2 6.43 us: half_sum(): summed(*terms).astype(bf16)]
  transfers between devices with their start and end apart: 7 -> 41, of which waited for: 6 -> 16; matrix products, arithmetic and copies ran while one was open for 9% -> 11% of each run, Pallas kernels for 0% -> 15%
where the time goes in v1:
time: 455 us; the launch traced here: 453 us
  waiting for transfers between devices  217 us (48%)
  Pallas kernels  94.3 us (21%)
  starting transfers between devices  74.2 us (16%)
  other arithmetic  49.2 us (11%)
  local copies, waits for them, and re-layouts  9.61 us (2%)
    ppermute x39, waiting for transfers between devices, send(): return lax.ppermute(value, ('row', 'col'), pairs)  204 us
    ppermute x39, starting transfers between devices, send(): return lax.ppermute(value, ('row', 'col'), pairs)  62.2 us
    pallas_call x4, Pallas kernels, terms(): pl.pallas_call(functools.partial(term_kernel, guard * width ** 0.5, 256,...  43.8 us
    pallas_call x2, Pallas kernels, step(): pl.pallas_call(functools.partial(step_kernel, rows_dev, tile, keep, base,...  31.6 us
    pallas_call x1, Pallas kernels, update(): pl.pallas_call(functools.partial(update_kernel, guard * width ** 0.5, 512...  18.9 us
    all_to_all x2, waiting for transfers between devices, exchange(): lax.all_to_all(value.reshape(paths, room, 2 * width), ('row', 'col'), spl...  12.9 us
    all_to_all x2, starting transfers between devices, exchange(): lax.all_to_all(value.reshape(paths, room, 2 * width), ('row', 'col'), spl...  12 us
    sub x2, other arithmetic, outer(): module - outer_rate * (outer_moment * following + average)  10 us
  transfers between devices with their start and end apart: 41, of which 16 were waited for; matrix products, arithmetic and copies ran while one was open for 11% of the time, Pallas kernels for 15%

profile of v1, /device:TPU:1, one launch (start us, length us, event | category | flops | bytes accessed | tf_op | source)
XLA Modules:
  0.0 453.1 jit_solution(967915112664972847)
XLA Ops:
  2.0 2.7 slice_bitcast_fusion
  4.8 2.1 fusion
  6.9 7.1 %all-to-all-start = ((bf16[32,8,4096]{2,1,0:T(8,128)(2,1)}), bf16[32,8,4096]{2,1,0:T(8,128)(2,1)}, u32[]{:S(2)}, u32[]{:S(2)}) async-start(bf16[32,8,4096]{2,1,0:T(8,128)(2,1)} %fusion), calls=%async_computation | async-start | bytes 4194304 | tf_op jit(solution)/shard_map/all_to_all | solution.py:386
  14.2 3.2 collective-permute-start.2
  17.5 2.5 convert_bitcast_fusion
  21.5 1.7 collective-permute-start.1
  23.2 1.6 collective-permute-start
  24.8 2.4 maximum_select_fusion
  32.4 42.0 %collective-permute-done.3.refs_11_ = bf16[512,1024]{1,0:T(8,128)(2,1)} collective-permute-done((bf16[512,1024]{1,0:T(8,128)(2,1)S(1)}, bf16[512,1024]{1,0:T(8,128)(2,1)}, u32[]{:S(2)}, u32[]{:S(2)}) %collective-permute-start.3) | collective-permute-done | bytes 1048608 | tf_op jit(solution)/shard_map/ppermute | solution.py:317
  75.9 1.7 collective-permute-start.7
  77.7 31.5 %collective-permute-done.4.refs_19_ = bf16[512,1024]{1,0:T(8,128)(2,1)} collective-permute-done((bf16[512,1024]{1,0:T(8,128)(2,1)S(1)}, bf16[512,1024]{1,0:T(8,128)(2,1)}, u32[]{:S(2)}, u32[]{:S(2)}) %collective-permute-start.4) | collective-permute-done | bytes 1048608 | tf_op jit(solution)/shard_map/ppermute | solution.py:317
  109.2 3.1 collective-permute-start.15
  112.4 3.1 collective-permute-start.16
  117.5 1.9 collective-permute-start.11
  119.4 2.2 collective-permute-start.19
  126.4 2.1 convolution_convert_fusion
  128.6 2.2 collective-permute-start.21
  130.8 3.1 collective-permute-start.20
  133.9 3.1 collective-permute-start.22
  137.0 9.1 %collective-permute-done.11 = bf16[512,1024]{1,0:T(8,128)(2,1)} collective-permute-done((bf16[512,1024]{1,0:T(8,128)(2,1)}, bf16[512,1024]{1,0:T(8,128)(2,1)}, u32[]{:S(2)}, u32[]{:S(2)}) %collective-permute-start.11) | collective-permute-done | bytes 1048608 | tf_op jit(solution)/shard_map/ppermute | solution.py:317
  146.1 1.9 collective-permute-start.17
  148.0 3.1 collective-permute-start.13
  151.1 4.4 collective-permute-done.22.refs_25_
  155.5 17.4 %collective-permute-done.17 = bf16[512,1024]{1,0:T(8,128)(2,1)S(1)} collective-permute-done((bf16[512,1024]{1,0:T(8,128)(2,1)}, bf16[512,1024]{1,0:T(8,128)(2,1)S(1)}, u32[]{:S(2)}, u32[]{:S(2)}) %collective-permute-start.17) | collective-permute-done | bytes 1048608 | tf_op jit(solution)/shard_map/ppermute | solution.py:317
  172.9 2.0 collective-permute-done.13
  174.9 1.9 collective-permute-start.23
  176.9 1.6 broadcast_select_fusion.1
  180.6 9.9 %collective-permute-done.23 = bf16[512,1024]{1,0:T(8,128)(2,1)S(1)} collective-permute-done((bf16[512,1024]{1,0:T(8,128)(2,1)S(1)}, bf16[512,1024]{1,0:T(8,128)(2,1)S(1)}, u32[]{:S(2)}, u32[]{:S(2)}) %collective-permute-start.23) | collective-permute-done | bytes 1048608 | tf_op jit(solution)/shard_map/ppermute | solution.py:317
  190.8 2.6 collective-permute-done.24.refs_9_
  194.4 4.8 %all-to-all-start.1 = ((bf16[32,8,4096]{2,1,0:T(8,128)(2,1)}), bf16[32,8,4096]{2,1,0:T(8,128)(2,1)S(1)}, u32[]{:S(2)}, u32[]{:S(2)}) async-start(bf16[32,8,4096]{2,1,0:T(8,128)(2,1)} %bitcast.27), calls=%async_computation.1 | async-start | bytes 4194304 | tf_op jit(solution)/shard_map/all_to_all | solution.py:386
  199.3 16.5 %shard_map.111 = (bf16[256,4096]{1,0:T(8,128)(2,1)}, bf16[256,4096]{1,0:T(8,128)(2,1)}, bf16[4096,2048]{1,0:T(8,128)(2,1)}) custom-call(s32[84]{0:T(128)} %stack.94.refs_0_.place_ref, bf16[256,4096]{1,0:T(8,128)(2,1)} %bitcast.21.refs_1_, bf16[512,1024]{1,0:T(8,128)(2,1)} %copy-done.21, bf16[512,1024]{1,0:T(8,128)(2,1)} %copy-done.37, ...), custom_call_target="tpu_custom_call" | custom-call | flops 16106127360 | bytes 16777216 | tf_op jit(solution)/shard_map/pallas_call | solution.py:142
  215.8 18.9 %shard_map.112.refs_2_.refs_3_ = bf16[4096,2048]{1,0:T(8,128)(2,1)} custom-call(bf16[256,4096]{1,0:T(8,128)(2,1)} %get-tuple-element.33.a_ref, bf16[256,4096]{1,0:T(8,128)(2,1)} %get-tuple-element.34.b_ref, bf16[4096,2048]{1,0:T(8,128)(2,1)} %get-tuple-element.36.p_ref), custom_call_target="tpu_custom_call" | custom-call | flops 25769803776 | bytes 33554432 | tf_op jit(solution)/shard_map/pallas_call | solution.py:176
  234.7 12.9 %all-to-all-done.1 = bf16[32,8,4096]{2,1,0:T(8,128)(2,1)S(1)} async-done(((bf16[32,8,4096]{2,1,0:T(8,128)(2,1)}), bf16[32,8,4096]{2,1,0:T(8,128)(2,1)S(1)}, u32[]{:S(2)}, u32[]{:S(2)}) %all-to-all-start.1) | async-done | bytes 2097184 | tf_op jit(solution)/shard_map/all_to_all | solution.py:386
  248.9 15.1 %shard_map.113 = (bf16[256,4096]{1,0:T(8,128)(2,1)}, bf16[256,4096]{1,0:T(8,128)(2,1)}) custom-call(s32[84]{0:T(128)} %stack.94.refs_0_.place_ref, bf16[256,4096]{1,0:T(8,128)(2,1)} %bitcast.74, bf16[4096,2048]{1,0:T(8,128)(2,1)} %shard_map.112.refs_2_.refs_3_, bf16[4096,2048]{1,0:T(8,128)(2,1)} %shard_map.112.refs_2_.refs_3_), custom_call_target="tpu_custom_call" | custom-call | flops 16106127360 | bytes 16777216 | tf_op jit(solution)/shard_map/pallas_call | solution.py:142
  264.0 11.0 %shard_map.114 = (bf16[1024,1024]{1,0:T(8,128)(2,1)}, bf16[1024,1024]{1,0:T(8,128)(2,1)}) custom-call(s32[84]{0:T(128)} %stack.94.refs_0_.place_ref, f32[2]{0:T(128)} %pad_maximum_fusion.weight_ref, bf16[256,4096]{1,0:T(8,128)(2,1)} %get-tuple-element.33.a_ref, bf16[256,4096]{1,0:T(8,128)(2,1)} %get-tuple-element.34.b_ref, ...), custom_call_target="tpu_custom_call" | custom-call | flops 1 | bytes 1 | tf_op jit(solution)/shard_map/pallas_call | solution.py:255
  275.5 10.9 %shard_map.115 = (bf16[1024,1024]{1,0:T(8,128)(2,1)}, bf16[1024,1024]{1,0:T(8,128)(2,1)}) custom-call(s32[84]{0:T(128)} %stack.94.refs_0_.place_ref, f32[2]{0:T(128)} %pad_maximum_fusion.weight_ref, bf16[256,4096]{1,0:T(8,128)(2,1)} %get-tuple-element.33.a_ref, bf16[256,4096]{1,0:T(8,128)(2,1)} %get-tuple-element.34.b_ref, ...), custom_call_target="tpu_custom_call" | custom-call | flops 1 | bytes 1 | tf_op jit(solution)/shard_map/pallas_call | solution.py:255
  286.5 3.4 add_convert_fusion.3
  289.9 1.9 collective-permute-start.26
  293.2 10.9 %shard_map.116 = (bf16[1024,1024]{1,0:T(8,128)(2,1)}, bf16[1024,1024]{1,0:T(8,128)(2,1)}) custom-call(s32[84]{0:T(128)} %stack.94.refs_0_.place_ref, f32[2]{0:T(128)} %pad_maximum_fusion.weight_ref, bf16[256,4096]{1,0:T(8,128)(2,1)} %get-tuple-element.33.a_ref, bf16[256,4096]{1,0:T(8,128)(2,1)} %get-tuple-element.34.b_ref, ...), custom_call_target="tpu_custom_call" | custom-call | flops 1 | bytes 1 | tf_op jit(solution)/shard_map/pallas_call | solution.py:255
  306.0 9.3 %collective-permute-done.26 = bf16[512,1024]{1,0:T(8,128)(2,1)S(1)} collective-permute-done((bf16[512,1024]{1,0:T(8,128)(2,1)}, bf16[512,1024]{1,0:T(8,128)(2,1)S(1)}, u32[]{:S(2)}, u32[]{:S(2)}) %collective-permute-start.26) | collective-permute-done | bytes 1048608 | tf_op jit(solution)/shard_map/ppermute | solution.py:317
  315.3 2.8 fusion.1
  318.1 4.0 collective-permute-start.27
  322.1 26.8 %collective-permute-done.29 = bf16[512,1024]{1,0:T(8,128)(2,1)S(1)} collective-permute-done((bf16[512,1024]{1,0:T(8,128)(2,1)}, bf16[512,1024]{1,0:T(8,128)(2,1)S(1)}, u32[]{:S(2)}, u32[]{:S(2)}) %collective-permute-start.29) | collective-permute-done | bytes 1048608 | tf_op jit(solution)/shard_map/ppermute | solution.py:317
  349.0 1.7 fusion.2
  350.7 1.9 collective-permute-start.30
  352.6 11.0 %shard_map.117 = (bf16[1024,1024]{1,0:T(8,128)(2,1)}, bf16[1024,1024]{1,0:T(8,128)(2,1)}) custom-call(s32[84]{0:T(128)} %stack.94.refs_0_.place_ref, f32[2]{0:T(128)} %pad_maximum_fusion.weight_ref, bf16[256,4096]{1,0:T(8,128)(2,1)} %get-tuple-element.33.a_ref, bf16[256,4096]{1,0:T(8,128)(2,1)} %get-tuple-element.34.b_ref, ...), custom_call_target="tpu_custom_call" | custom-call | flops 1 | bytes 1 | tf_op jit(solution)/shard_map/pallas_call | solution.py:255
  363.6 2.1 add_convert_fusion
  365.7 1.6 collective-permute-start.36
  367.3 1.6 add_convert_fusion.1
  369.5 2.1 convert_select_fusion.1
  371.5 6.8 %collective-permute-done.30 = bf16[512,1024]{1,0:T(8,128)(2,1)} collective-permute-done((bf16[512,1024]{1,0:T(8,128)(2,1)}, bf16[512,1024]{1,0:T(8,128)(2,1)}, u32[]{:S(2)}, u32[]{:S(2)}) %collective-permute-start.30) | collective-permute-done | bytes 1048608 | tf_op jit(solution)/shard_map/ppermute | solution.py:317
  378.3 2.1 convert_select_fusion
  380.4 9.8 %collective-permute-done.36 = bf16[512,1024]{1,0:T(8,128)(2,1)S(1)} collective-permute-done((bf16[512,1024]{1,0:T(8,128)(2,1)S(1)}, bf16[512,1024]{1,0:T(8,128)(2,1)S(1)}, u32[]{:S(2)}, u32[]{:S(2)}) %collective-permute-start.36) | collective-permute-done | bytes 1048608 | tf_op jit(solution)/shard_map/ppermute | solution.py:317
  390.1 3.2 fusion.4
  393.3 2.6 collective-permute-start.37
  395.9 3.2 fusion.3
  399.1 2.4 collective-permute-start.33
  401.5 7.3 %multiply_subtract_fusion = (f32[1,512,2048]{2,1,0:T(8,128)}, f32[1,512,2048]{2,1,0:T(8,128)}) fusion(f32[1,512,2048]{2,1,0:T(8,128)S(1)} %copy-done, f32[512,1024]{1,0:T(8,128)S(1)} %convert_select_fusion, f32[512,1024]{1,0:T(8,128)S(1)} %convert_select_fusion.1, f32[1,512,2048]{2,1,0:T(8,128)} %param.14), kind=kLoop, calls=%fused_computation.4 | loop fusion | flops 7340032 | bytes 20971520 | tf_op jit(solution)/shard_map/sub | solution.py:512
  408.9 2.8 convert_add_fusion
  413.3 4.9 %collective-permute-done.33 = bf16[512,1024]{1,0:T(8,128)(2,1)} collective-permute-done((bf16[512,1024]{1,0:T(8,128)(2,1)}, bf16[512,1024]{1,0:T(8,128)(2,1)}, u32[]{:S(2)}, u32[]{:S(2)}) %collective-permute-start.33) | collective-permute-done | bytes 1048608 | tf_op jit(solution)/shard_map/ppermute | solution.py:317
  418.2 2.4 convert_add_fusion.2
  422.0 17.5 %collective-permute-done.38 = bf16[256,1024]{1,0:T(8,128)(2,1)S(1)} collective-permute-done((bf16[256,1024]{1,0:T(8,128)(2,1)S(1)}, bf16[256,1024]{1,0:T(8,128)(2,1)S(1)}, u32[]{:S(2)}, u32[]{:S(2)}) %collective-permute-start.38) | collective-permute-done | bytes 524320 | tf_op jit(solution)/shard_map/ppermute | solution.py:317
  439.8 10.4 %collective-permute-done.34 = bf16[256,1024]{1,0:T(8,128)(2,1)S(1)} collective-permute-done((bf16[256,1024]{1,0:T(8,128)(2,1)S(1)}, bf16[256,1024]{1,0:T(8,128)(2,1)S(1)}, u32[]{:S(2)}, u32[]{:S(2)}) %collective-permute-start.34) | collective-permute-done | bytes 524320 | tf_op jit(solution)/shard_map/ppermute | solution.py:317
  450.4 2.7 multiply_subtract_fusion.1
  (153 shorter events, 26.2 us)
Async XLA Ops:
  6.9 7.2 %copy-start.1 = (f32[1,256,2048]{2,1,0:T(8,128)S(1)}, f32[1,256,2048]{2,1,0:T(8,128)}, u32[]{:S(2)}) copy-start(f32[1,256,2048]{2,1,0:T(8,128)} %param.13) | copy-start | bytes 6291460
  6.9 110.6 %all-to-all-start = ((bf16[32,8,4096]{2,1,0:T(8,128)(2,1)}), bf16[32,8,4096]{2,1,0:T(8,128)(2,1)}, u32[]{:S(2)}, u32[]{:S(2)}) async-start(bf16[32,8,4096]{2,1,0:T(8,128)(2,1)} %fusion), calls=%async_computation | async-start | bytes 4194304 | tf_op jit(solution)/shard_map/all_to_all | solution.py:386
  14.2 10.6 %collective-permute-start.2 = (bf16[256,2048]{1,0:T(8,128)(2,1)S(1)}, bf16[256,2048]{1,0:T(8,128)(2,1)}, u32[]{:S(2)}, u32[]{:S(2)}) collective-permute-start(bf16[256,2048]{1,0:T(8,128)(2,1)S(1)} %convert_bitcast_fusion.1), channel_id=1, source_target_pairs={{2,6},{3,7},{4,0},{5,1},{10,14},{11,15},{12,8},{13,9},{18,22},{19,... | collective-permute-start | bytes 3145736 | tf_op jit(solution)/shard_map/ppermute | solution.py:317
  21.5 8.8 %collective-permute-start.1 = (bf16[512,1024]{1,0:T(8,128)(2,1)}, bf16[512,1024]{1,0:T(8,128)(2,1)}, u32[]{:S(2)}, u32[]{:S(2)}) collective-permute-start(bf16[512,1024]{1,0:T(8,128)(2,1)} %get-tuple-element.31), channel_id=1, source_target_pairs={{0,1},{1,0},{6,7},{7,6},{8,9},{9,8},{14,15},{15,14},{16,17},{17,16... | collective-permute-start | bytes 3145736 | tf_op jit(solution)/shard_map/ppermute | solution.py:317
  23.2 7.9 %collective-permute-start = (bf16[512,1024]{1,0:T(8,128)(2,1)}, bf16[512,1024]{1,0:T(8,128)(2,1)}, u32[]{:S(2)}, u32[]{:S(2)}) collective-permute-start(bf16[512,1024]{1,0:T(8,128)(2,1)} %get-tuple-element.30), channel_id=1, source_target_pairs={{0,1},{1,0},{6,7},{7,6},{8,9},{9,8},{14,15},{15,14},{16,17},{17,16... | collective-permute-start | bytes 3145736 | tf_op jit(solution)/shard_map/ppermute | solution.py:317
  27.2 94.5 %copy-start.27 = (s32[8,4]{0,1:T(4,128)S(1)}, s32[8,4]{0,1:T(4,128)}, u32[]{:S(2)}) copy-start(s32[8,4]{0,1:T(4,128)} %param.11) | copy-start | bytes 388
  27.2 99.2 %copy-start.18 = (bf16[128,2048]{1,0:T(8,128)(2,1)S(1)}, bf16[128,2048]{1,0:T(8,128)(2,1)}, u32[]{:S(2)}) copy-start(bf16[128,2048]{1,0:T(8,128)(2,1)} %get-tuple-element.71) | copy-start | bytes 1572868
  27.2 99.2 %copy-start.19 = (bf16[128,2048]{1,0:T(8,128)(2,1)S(1)}, bf16[128,2048]{1,0:T(8,128)(2,1)}, u32[]{:S(2)}) copy-start(bf16[128,2048]{1,0:T(8,128)(2,1)} %get-tuple-element.78) | copy-start | bytes 1572868
  27.4 84.9 %copy-start.26 = (bf16[512,1024]{1,0:T(8,128)(2,1)}, bf16[512,1024]{1,0:T(8,128)(2,1)S(1)}, u32[]{:S(2)}) copy-start(bf16[512,1024]{1,0:T(8,128)(2,1)S(1)} %get-tuple-element.66.refs_10_) | copy-start | bytes 3145732
  27.4 47.0 %collective-permute-start.3 = (bf16[512,1024]{1,0:T(8,128)(2,1)S(1)}, bf16[512,1024]{1,0:T(8,128)(2,1)}, u32[]{:S(2)}, u32[]{:S(2)}) collective-permute-start(bf16[512,1024]{1,0:T(8,128)(2,1)S(1)} %get-tuple-element.66.refs_10_), channel_id=1, source_target_pairs={{0,2},{1,3},{6,4},{7,5},{8,10},{9,11},{14,12},{15,13},{16,18},{17,... | collective-permute-start | bytes 3145736 | tf_op jit(solution)/shard_map/ppermute | solution.py:317
  28.9 46.3 %collective-permute-start.8 = (bf16[512,1024]{1,0:T(8,128)(2,1)S(1)}, bf16[512,1024]{1,0:T(8,128)(2,1)S(1)}, u32[]{:S(2)}, u32[]{:S(2)}) collective-permute-start(bf16[512,1024]{1,0:T(8,128)(2,1)S(1)} %get-tuple-element.65.refs_18_), channel_id=1, source_target_pairs={{0,16},{1,17},{6,22},{7,23},{8,24},{9,25},{14,30},{15,31},{16,0},{... | collective-permute-start | bytes 3145736 | tf_op jit(solution)/shard_map/ppermute | solution.py:317
  29.6 46.3 %collective-permute-start.5 = (bf16[512,1024]{1,0:T(8,128)(2,1)S(1)}, bf16[512,1024]{1,0:T(8,128)(2,1)S(1)}, u32[]{:S(2)}, u32[]{:S(2)}) collective-permute-start(bf16[512,1024]{1,0:T(8,128)(2,1)S(1)} %get-tuple-element.66.refs_10_), channel_id=1, source_target_pairs={{0,8},{1,9},{6,14},{7,15},{8,0},{9,1},{14,6},{15,7},{16,24},{17,25... | collective-permute-start | bytes 3145736 | tf_op jit(solution)/shard_map/ppermute | solution.py:317
  30.3 82.0 %collective-permute-start.9 = (bf16[512,1024]{1,0:T(8,128)(2,1)S(1)}, bf16[512,1024]{1,0:T(8,128)(2,1)S(1)}, u32[]{:S(2)}, u32[]{:S(2)}) collective-permute-start(bf16[512,1024]{1,0:T(8,128)(2,1)S(1)} %get-tuple-element.65.refs_18_), channel_id=1, source_target_pairs={{0,8},{1,9},{6,14},{7,15},{8,0},{9,1},{14,6},{15,7},{16,24},{17,25... | collective-permute-start | bytes 3145736 | tf_op jit(solution)/shard_map/ppermute | solution.py:317
  31.1 78.1 %collective-permute-start.4 = (bf16[512,1024]{1,0:T(8,128)(2,1)S(1)}, bf16[512,1024]{1,0:T(8,128)(2,1)}, u32[]{:S(2)}, u32[]{:S(2)}) collective-permute-start(bf16[512,1024]{1,0:T(8,128)(2,1)S(1)} %get-tuple-element.65.refs_18_), channel_id=1, source_target_pairs={{0,2},{1,3},{6,4},{7,5},{8,10},{9,11},{14,12},{15,13},{16,18},{17,... | collective-permute-start | bytes 3145736 | tf_op jit(solution)/shard_map/ppermute | solution.py:317
  74.4 41.0 %collective-permute-start.6 = (bf16[512,1024]{1,0:T(8,128)(2,1)S(1)}, bf16[512,1024]{1,0:T(8,128)(2,1)S(1)}, u32[]{:S(2)}, u32[]{:S(2)}) collective-permute-start(bf16[512,1024]{1,0:T(8,128)(2,1)S(1)} %get-tuple-element.66.refs_10_), channel_id=1, source_target_pairs={{0,16},{1,17},{6,22},{7,23},{8,24},{9,25},{14,30},{15,31},{16,0},{... | collective-permute-start | bytes 3145736 | tf_op jit(solution)/shard_map/ppermute | solution.py:317
  75.2 40.3 %copy-start.28 = (bf16[512,1024]{1,0:T(8,128)(2,1)}, bf16[512,1024]{1,0:T(8,128)(2,1)S(1)}, u32[]{:S(2)}) copy-start(bf16[512,1024]{1,0:T(8,128)(2,1)S(1)} %collective-permute-done.8.refs_22_) | copy-start | bytes 3145732
  75.2 40.3 %collective-permute-start.10 = (bf16[512,1024]{1,0:T(8,128)(2,1)S(1)}, bf16[512,1024]{1,0:T(8,128)(2,1)S(1)}, u32[]{:S(2)}, u32[]{:S(2)}) collective-permute-start(bf16[512,1024]{1,0:T(8,128)(2,1)S(1)} %collective-permute-done.8.refs_22_), channel_id=1, source_target_pairs={{0,8},{1,9},{6,14},{7,15},{8,0},{9,1},{14,6},{15,7},{16,24},{17,25... | collective-permute-start | bytes 3145736 | tf_op jit(solution)/shard_map/ppermute | solution.py:317
  75.9 39.6 %copy-start.29 = (bf16[512,1024]{1,0:T(8,128)(2,1)}, bf16[512,1024]{1,0:T(8,128)(2,1)S(1)}, u32[]{:S(2)}) copy-start(bf16[512,1024]{1,0:T(8,128)(2,1)S(1)} %collective-permute-done.5.refs_12_) | copy-start | bytes 3145732
  75.9 41.5 %collective-permute-start.7 = (bf16[512,1024]{1,0:T(8,128)(2,1)S(1)}, bf16[512,1024]{1,0:T(8,128)(2,1)}, u32[]{:S(2)}, u32[]{:S(2)}) collective-permute-start(bf16[512,1024]{1,0:T(8,128)(2,1)S(1)} %collective-permute-done.5.refs_12_), channel_id=1, source_target_pairs={{0,16},{1,17},{6,22},{7,23},{8,24},{9,25},{14,30},{15,31},{16,0},{... | collective-permute-start | bytes 3145736 | tf_op jit(solution)/shard_map/ppermute | solution.py:317
  109.2 21.5 %collective-permute-start.15 = (bf16[512,1024]{1,0:T(8,128)(2,1)}, bf16[512,1024]{1,0:T(8,128)(2,1)}, u32[]{:S(2)}, u32[]{:S(2)}) collective-permute-start(bf16[512,1024]{1,0:T(8,128)(2,1)} %collective-permute-done.3.refs_11_), channel_id=1, source_target_pairs={{2,10},{3,11},{4,12},{5,13},{10,2},{11,3},{12,4},{13,5},{18,26},{1... | collective-permute-start | bytes 3145736 | tf_op jit(solution)/shard_map/ppermute | solution.py:317
  112.4 21.5 %collective-permute-start.16 = (bf16[512,1024]{1,0:T(8,128)(2,1)}, bf16[512,1024]{1,0:T(8,128)(2,1)}, u32[]{:S(2)}, u32[]{:S(2)}) collective-permute-start(bf16[512,1024]{1,0:T(8,128)(2,1)} %collective-permute-done.4.refs_19_), channel_id=1, source_target_pairs={{2,18},{3,19},{4,20},{5,21},{10,26},{11,27},{12,28},{13,29},{18,2}... | collective-permute-start | bytes 3145736 | tf_op jit(solution)/shard_map/ppermute | solution.py:317
  117.5 28.6 %collective-permute-start.11 = (bf16[512,1024]{1,0:T(8,128)(2,1)}, bf16[512,1024]{1,0:T(8,128)(2,1)}, u32[]{:S(2)}, u32[]{:S(2)}) collective-permute-start(bf16[512,1024]{1,0:T(8,128)(2,1)} %get-tuple-element.30), channel_id=1, source_target_pairs={{2,4},{3,5},{4,2},{5,3},{10,12},{11,13},{12,10},{13,11},{18,20},{1... | collective-permute-start | bytes 3145736 | tf_op jit(solution)/shard_map/ppermute | solution.py:317
  119.4 28.6 %collective-permute-start.19 = (bf16[512,1024]{1,0:T(8,128)(2,1)}, bf16[512,1024]{1,0:T(8,128)(2,1)}, u32[]{:S(2)}, u32[]{:S(2)}) collective-permute-start(bf16[512,1024]{1,0:T(8,128)(2,1)} %collective-permute-done.3.refs_11_), channel_id=1, source_target_pairs={{2,18},{3,19},{4,20},{5,21},{10,26},{11,27},{12,28},{13,29},{18,2}... | collective-permute-start | bytes 3145736 | tf_op jit(solution)/shard_map/ppermute | solution.py:317
  128.6 22.5 %collective-permute-start.21 = (bf16[512,1024]{1,0:T(8,128)(2,1)}, bf16[512,1024]{1,0:T(8,128)(2,1)S(1)}, u32[]{:S(2)}, u32[]{:S(2)}) collective-permute-start(bf16[512,1024]{1,0:T(8,128)(2,1)} %collective-permute-done.4.refs_19_), channel_id=1, source_target_pairs={{2,10},{3,11},{4,12},{5,13},{10,2},{11,3},{12,4},{13,5},{18,26},{1... | collective-permute-start | bytes 3145736 | tf_op jit(solution)/shard_map/ppermute | solution.py:317
  130.8 20.4 %collective-permute-start.20 = (bf16[512,1024]{1,0:T(8,128)(2,1)}, bf16[512,1024]{1,0:T(8,128)(2,1)S(1)}, u32[]{:S(2)}, u32[]{:S(2)}) collective-permute-start(bf16[512,1024]{1,0:T(8,128)(2,1)} %collective-permute-done.15.refs_13_), channel_id=1, source_target_pairs={{2,18},{3,19},{4,20},{5,21},{10,26},{11,27},{12,28},{13,29},{18,2}... | collective-permute-start | bytes 3145736 | tf_op jit(solution)/shard_map/ppermute | solution.py:317
  133.9 21.7 %collective-permute-start.22 = (bf16[512,1024]{1,0:T(8,128)(2,1)}, bf16[512,1024]{1,0:T(8,128)(2,1)S(1)}, u32[]{:S(2)}, u32[]{:S(2)}) collective-permute-start(bf16[512,1024]{1,0:T(8,128)(2,1)} %collective-permute-done.16.refs_23_), channel_id=1, source_target_pairs={{2,10},{3,11},{4,12},{5,13},{10,2},{11,3},{12,4},{13,5},{18,26},{1... | collective-permute-start | bytes 3145736 | tf_op jit(solution)/shard_map/ppermute | solution.py:317
  146.1 26.8 %collective-permute-start.17 = (bf16[512,1024]{1,0:T(8,128)(2,1)}, bf16[512,1024]{1,0:T(8,128)(2,1)S(1)}, u32[]{:S(2)}, u32[]{:S(2)}) collective-permute-start(bf16[512,1024]{1,0:T(8,128)(2,1)} %get-tuple-element.31), channel_id=1, source_target_pairs={{2,4},{3,5},{4,2},{5,3},{10,12},{11,13},{12,10},{13,11},{18,20},{1... | collective-permute-start | bytes 3145736 | tf_op jit(solution)/shard_map/ppermute | solution.py:317
  148.0 26.9 %collective-permute-start.13 = (bf16[512,1024]{1,0:T(8,128)(2,1)}, bf16[512,1024]{1,0:T(8,128)(2,1)S(1)}, u32[]{:S(2)}, u32[]{:S(2)}) collective-permute-start(bf16[512,1024]{1,0:T(8,128)(2,1)} %collective-permute-done.11), channel_id=1, source_target_pairs={{2,3},{3,2},{4,5},{5,4},{10,11},{11,10},{12,13},{13,12},{18,19},{1... | collective-permute-start | bytes 3145736 | tf_op jit(solution)/shard_map/ppermute | solution.py:317
  151.1 23.8 %copy-start.33 = (bf16[512,1024]{1,0:T(8,128)(2,1)}, bf16[512,1024]{1,0:T(8,128)(2,1)S(1)}, u32[]{:S(2)}) copy-start(bf16[512,1024]{1,0:T(8,128)(2,1)S(1)} %collective-permute-done.21.refs_21_) | copy-start | bytes 3145732
  151.1 23.8 %copy-start.34 = (bf16[512,1024]{1,0:T(8,128)(2,1)}, bf16[512,1024]{1,0:T(8,128)(2,1)S(1)}, u32[]{:S(2)}) copy-start(bf16[512,1024]{1,0:T(8,128)(2,1)S(1)} %collective-permute-done.20.refs_17_) | copy-start | bytes 3145732
  155.5 19.4 %copy-start.35 = (bf16[512,1024]{1,0:T(8,128)(2,1)}, bf16[512,1024]{1,0:T(8,128)(2,1)S(1)}, u32[]{:S(2)}) copy-start(bf16[512,1024]{1,0:T(8,128)(2,1)S(1)} %collective-permute-done.22.refs_25_) | copy-start | bytes 3145732
  174.9 15.5 %collective-permute-start.23 = (bf16[512,1024]{1,0:T(8,128)(2,1)S(1)}, bf16[512,1024]{1,0:T(8,128)(2,1)S(1)}, u32[]{:S(2)}, u32[]{:S(2)}) collective-permute-start(bf16[512,1024]{1,0:T(8,128)(2,1)S(1)} %collective-permute-done.17), channel_id=1, source_target_pairs={{2,3},{3,2},{4,5},{5,4},{10,11},{11,10},{12,13},{13,12},{18,19},{1... | collective-permute-start | bytes 3145736 | tf_op jit(solution)/shard_map/ppermute | solution.py:317
  178.4 12.2 %copy-start.20 = (bf16[512,1024]{1,0:T(8,128)(2,1)}, bf16[512,1024]{1,0:T(8,128)(2,1)S(1)}, u32[]{:S(2)}) copy-start(bf16[512,1024]{1,0:T(8,128)(2,1)S(1)} %get-tuple-element.63.refs_6_) | copy-start | bytes 3145732
  178.4 12.2 %copy-start.21 = (bf16[512,1024]{1,0:T(8,128)(2,1)}, bf16[512,1024]{1,0:T(8,128)(2,1)S(1)}, u32[]{:S(2)}) copy-start(bf16[512,1024]{1,0:T(8,128)(2,1)S(1)} %get-tuple-element.64.refs_2_) | copy-start | bytes 3145732
  178.5 12.3 %collective-permute-start.18 = (bf16[512,1024]{1,0:T(8,128)(2,1)S(1)}, bf16[512,1024]{1,0:T(8,128)(2,1)S(1)}, u32[]{:S(2)}, u32[]{:S(2)}) collective-permute-start(bf16[512,1024]{1,0:T(8,128)(2,1)S(1)} %get-tuple-element.63.refs_6_), channel_id=1, source_target_pairs={{0,4},{1,5},{2,6},{3,7},{4,0},{5,1},{6,2},{7,3},{8,12},{9,13},{10,... | collective-permute-start | bytes 3145736 | tf_op jit(solution)/shard_map/ppermute | solution.py:317
  178.5 12.2 %collective-permute-start.12 = (bf16[512,1024]{1,0:T(8,128)(2,1)S(1)}, bf16[512,1024]{1,0:T(8,128)(2,1)S(1)}, u32[]{:S(2)}, u32[]{:S(2)}) collective-permute-start(bf16[512,1024]{1,0:T(8,128)(2,1)S(1)} %get-tuple-element.64.refs_2_), channel_id=1, source_target_pairs={{0,4},{1,5},{2,6},{3,7},{4,0},{5,1},{6,2},{7,3},{8,12},{9,13},{10,... | collective-permute-start | bytes 3145736 | tf_op jit(solution)/shard_map/ppermute | solution.py:317
  179.2 15.3 %copy-start.23 = (bf16[512,1024]{1,0:T(8,128)(2,1)}, bf16[512,1024]{1,0:T(8,128)(2,1)S(1)}, u32[]{:S(2)}) copy-start(bf16[512,1024]{1,0:T(8,128)(2,1)S(1)} %broadcast_select_fusion.2.refs_4_) | copy-start | bytes 3145732
  179.2 11.6 %collective-permute-start.14 = (bf16[512,1024]{1,0:T(8,128)(2,1)S(1)}, bf16[512,1024]{1,0:T(8,128)(2,1)S(1)}, u32[]{:S(2)}, u32[]{:S(2)}) collective-permute-start(bf16[512,1024]{1,0:T(8,128)(2,1)S(1)} %broadcast_select_fusion.2.refs_4_), channel_id=1, source_target_pairs={{0,4},{1,5},{2,6},{3,7},{4,0},{5,1},{6,2},{7,3},{8,12},{9,13},{10,... | collective-permute-start | bytes 3145736 | tf_op jit(solution)/shard_map/ppermute | solution.py:317
  190.7 2.7 collective-permute-start.24
  194.4 53.1 %all-to-all-start.1 = ((bf16[32,8,4096]{2,1,0:T(8,128)(2,1)}), bf16[32,8,4096]{2,1,0:T(8,128)(2,1)S(1)}, u32[]{:S(2)}, u32[]{:S(2)}) async-start(bf16[32,8,4096]{2,1,0:T(8,128)(2,1)} %bitcast.27), calls=%async_computation.1 | async-start | bytes 4194304 | tf_op jit(solution)/shard_map/all_to_all | solution.py:386
  274.9 11.5 %collective-permute-start.25 = (bf16[1024,1024]{1,0:T(8,128)(2,1)}, bf16[1024,1024]{1,0:T(8,128)(2,1)S(1)}, u32[]{:S(2)}, u32[]{:S(2)}) collective-permute-start(bf16[1024,1024]{1,0:T(8,128)(2,1)} %get-tuple-element.39), channel_id=1, source_target_pairs={{0,4},{1,5},{2,6},{3,7},{4,0},{5,1},{6,2},{7,3},{8,12},{9,13},{10,... | collective-permute-start | bytes 6291464 | tf_op jit(solution)/shard_map/ppermute | solution.py:317
  275.0 16.8 %collective-permute-start.28 = (bf16[1024,1024]{1,0:T(8,128)(2,1)}, bf16[1024,1024]{1,0:T(8,128)(2,1)S(1)}, u32[]{:S(2)}, u32[]{:S(2)}) collective-permute-start(bf16[1024,1024]{1,0:T(8,128)(2,1)} %get-tuple-element.43), channel_id=1, source_target_pairs={{0,4},{1,5},{2,6},{3,7},{4,0},{5,1},{6,2},{7,3},{8,12},{9,13},{10,... | collective-permute-start | bytes 6291464 | tf_op jit(solution)/shard_map/ppermute | solution.py:317
  286.5 28.8 %copy-start.4 = (bf16[1024,1024]{1,0:T(8,128)(2,1)}, bf16[1024,1024]{1,0:T(8,128)(2,1)S(1)}, u32[]{:S(2)}) copy-start(bf16[1024,1024]{1,0:T(8,128)(2,1)S(1)} %collective-permute-done.25) | copy-start | bytes 6291460
  289.9 25.4 %collective-permute-start.26 = (bf16[512,1024]{1,0:T(8,128)(2,1)}, bf16[512,1024]{1,0:T(8,128)(2,1)S(1)}, u32[]{:S(2)}, u32[]{:S(2)}) collective-permute-start(bf16[512,1024]{1,0:T(8,128)(2,1)} %add_convert_fusion.3), channel_id=1, source_target_pairs={{0,1},{1,0},{2,3},{3,2},{4,5},{5,4},{6,7},{7,6},{8,9},{9,8},{10,11... | collective-permute-start | bytes 3145736 | tf_op jit(solution)/shard_map/ppermute | solution.py:317
  304.2 59.4 %collective-permute-start.35 = (bf16[1024,1024]{1,0:T(8,128)(2,1)}, bf16[1024,1024]{1,0:T(8,128)(2,1)}, u32[]{:S(2)}, u32[]{:S(2)}) collective-permute-start(bf16[1024,1024]{1,0:T(8,128)(2,1)} %get-tuple-element.52), channel_id=1, source_target_pairs={{0,16},{1,17},{2,18},{3,19},{4,20},{5,21},{6,22},{7,23},{8,24},{9,... | collective-permute-start | bytes 6291464 | tf_op jit(solution)/shard_map/ppermute | solution.py:317
  304.5 62.8 %collective-permute-start.31 = (bf16[1024,1024]{1,0:T(8,128)(2,1)}, bf16[1024,1024]{1,0:T(8,128)(2,1)}, u32[]{:S(2)}, u32[]{:S(2)}) collective-permute-start(bf16[1024,1024]{1,0:T(8,128)(2,1)} %get-tuple-element.45), channel_id=1, source_target_pairs={{0,8},{1,9},{2,10},{3,11},{4,12},{5,13},{6,14},{7,15},{8,0},{9,1},... | collective-permute-start | bytes 6291464 | tf_op jit(solution)/shard_map/ppermute | solution.py:317
  305.5 43.5 %collective-permute-start.29 = (bf16[512,1024]{1,0:T(8,128)(2,1)}, bf16[512,1024]{1,0:T(8,128)(2,1)S(1)}, u32[]{:S(2)}, u32[]{:S(2)}) collective-permute-start(bf16[512,1024]{1,0:T(8,128)(2,1)} %add_convert_fusion.2), channel_id=1, source_target_pairs={{0,1},{1,0},{2,3},{3,2},{4,5},{5,4},{6,7},{7,6},{8,9},{9,8},{10,11... | collective-permute-start | bytes 3145736 | tf_op jit(solution)/shard_map/ppermute | solution.py:317
  318.1 47.6 %collective-permute-start.27 = (bf16[512,1024]{1,0:T(8,128)(2,1)}, bf16[512,1024]{1,0:T(8,128)(2,1)S(1)}, u32[]{:S(2)}, u32[]{:S(2)}) collective-permute-start(bf16[512,1024]{1,0:T(8,128)(2,1)} %fusion.1), channel_id=1, source_target_pairs={{2,4},{3,5},{4,2},{5,3},{10,12},{11,13},{12,10},{13,11},{18,20},{1... | collective-permute-start | bytes 3145736 | tf_op jit(solution)/shard_map/ppermute | solution.py:317
  350.7 27.6 %collective-permute-start.30 = (bf16[512,1024]{1,0:T(8,128)(2,1)}, bf16[512,1024]{1,0:T(8,128)(2,1)}, u32[]{:S(2)}, u32[]{:S(2)}) collective-permute-start(bf16[512,1024]{1,0:T(8,128)(2,1)} %fusion.2), channel_id=1, source_target_pairs={{2,4},{3,5},{4,2},{5,3},{10,12},{11,13},{12,10},{13,11},{18,20},{1... | collective-permute-start | bytes 3145736 | tf_op jit(solution)/shard_map/ppermute | solution.py:317
  363.6 5.9 %copy-start.6 = (bf16[1024,1024]{1,0:T(8,128)(2,1)S(1)}, bf16[1024,1024]{1,0:T(8,128)(2,1)}, u32[]{:S(2)}) copy-start(bf16[1024,1024]{1,0:T(8,128)(2,1)} %get-tuple-element.41) | copy-start | bytes 6291460
  365.7 24.4 %collective-permute-start.36 = (bf16[512,1024]{1,0:T(8,128)(2,1)S(1)}, bf16[512,1024]{1,0:T(8,128)(2,1)S(1)}, u32[]{:S(2)}, u32[]{:S(2)}) collective-permute-start(bf16[512,1024]{1,0:T(8,128)(2,1)S(1)} %add_convert_fusion), channel_id=1, source_target_pairs={{0,8},{1,9},{2,10},{3,11},{4,12},{5,13},{6,14},{7,15},{8,0},{9,1},... | collective-permute-start | bytes 3145736 | tf_op jit(solution)/shard_map/ppermute | solution.py:317
  369.0 9.3 %copy-start.11 = (bf16[512,1024]{1,0:T(8,128)(2,1)S(1)}, bf16[512,1024]{1,0:T(8,128)(2,1)}, u32[]{:S(2)}) copy-start(bf16[512,1024]{1,0:T(8,128)(2,1)} %copy-done.10) | copy-start | bytes 3145732
  369.0 26.9 %collective-permute-start.32 = (bf16[512,1024]{1,0:T(8,128)(2,1)S(1)}, bf16[512,1024]{1,0:T(8,128)(2,1)S(1)}, u32[]{:S(2)}, u32[]{:S(2)}) collective-permute-start(bf16[512,1024]{1,0:T(8,128)(2,1)S(1)} %add_convert_fusion.1), channel_id=1, source_target_pairs={{0,16},{1,17},{2,18},{3,19},{4,20},{5,21},{6,22},{7,23},{8,24},{9,... | collective-permute-start | bytes 3145736 | tf_op jit(solution)/shard_map/ppermute | solution.py:317
  371.5 18.6 %copy-start.9 = (bf16[1024,1024]{1,0:T(8,128)(2,1)S(1)}, bf16[1024,1024]{1,0:T(8,128)(2,1)}, u32[]{:S(2)}) copy-start(bf16[1024,1024]{1,0:T(8,128)(2,1)} %get-tuple-element.51) | copy-start | bytes 6291460
  393.3 8.2 %copy-start = (f32[1,512,2048]{2,1,0:T(8,128)S(1)}, f32[1,512,2048]{2,1,0:T(8,128)}, u32[]{:S(2)}) copy-start(f32[1,512,2048]{2,1,0:T(8,128)} %param.12) | copy-start | bytes 12582916
  393.3 15.5 %collective-permute-start.37 = (bf16[512,1024]{1,0:T(8,128)(2,1)}, bf16[512,1024]{1,0:T(8,128)(2,1)}, u32[]{:S(2)}, u32[]{:S(2)}) collective-permute-start(bf16[512,1024]{1,0:T(8,128)(2,1)} %fusion.4), channel_id=1, source_target_pairs={{2,0},{3,1},{4,6},{5,7},{10,8},{11,9},{12,14},{13,15},{18,16},{19,... | collective-permute-start | bytes 3145736 | tf_op jit(solution)/shard_map/ppermute | solution.py:317
  399.1 9.8 %copy-start.15 = (bf16[512,1024]{1,0:T(8,128)(2,1)S(1)}, bf16[512,1024]{1,0:T(8,128)(2,1)}, u32[]{:S(2)}) copy-start(bf16[512,1024]{1,0:T(8,128)(2,1)} %copy-done.14) | copy-start | bytes 3145732
  399.1 19.1 %collective-permute-start.33 = (bf16[512,1024]{1,0:T(8,128)(2,1)}, bf16[512,1024]{1,0:T(8,128)(2,1)}, u32[]{:S(2)}, u32[]{:S(2)}) collective-permute-start(bf16[512,1024]{1,0:T(8,128)(2,1)} %fusion.3), channel_id=1, source_target_pairs={{2,0},{3,1},{4,6},{5,7},{10,8},{11,9},{12,14},{13,15},{18,16},{19,... | collective-permute-start | bytes 3145736 | tf_op jit(solution)/shard_map/ppermute | solution.py:317
  408.9 9.3 %copy-start.8 = (bf16[1024,1024]{1,0:T(8,128)(2,1)S(1)}, bf16[1024,1024]{1,0:T(8,128)(2,1)}, u32[]{:S(2)}) copy-start(bf16[1024,1024]{1,0:T(8,128)(2,1)} %get-tuple-element.47) | copy-start | bytes 6291460
  411.7 6.5 %copy-start.13 = (bf16[512,1024]{1,0:T(8,128)(2,1)S(1)}, bf16[512,1024]{1,0:T(8,128)(2,1)}, u32[]{:S(2)}) copy-start(bf16[512,1024]{1,0:T(8,128)(2,1)} %copy-done.12) | copy-start | bytes 3145732
  411.9 27.6 %collective-permute-start.38 = (bf16[256,1024]{1,0:T(8,128)(2,1)S(1)}, bf16[256,1024]{1,0:T(8,128)(2,1)S(1)}, u32[]{:S(2)}, u32[]{:S(2)}) collective-permute-start(bf16[256,1024]{1,0:T(8,128)(2,1)S(1)} %select_convert_fusion), channel_id=1, source_target_pairs={{0,4},{1,5},{6,2},{7,3},{8,12},{9,13},{14,10},{15,11},{16,20},{17,... | collective-permute-start | bytes 1572872 | tf_op jit(solution)/shard_map/ppermute | solution.py:317
  420.7 29.4 %collective-permute-start.34 = (bf16[256,1024]{1,0:T(8,128)(2,1)S(1)}, bf16[256,1024]{1,0:T(8,128)(2,1)S(1)}, u32[]{:S(2)}, u32[]{:S(2)}) collective-permute-start(bf16[256,1024]{1,0:T(8,128)(2,1)S(1)} %select_convert_fusion.1), channel_id=1, source_target_pairs={{0,4},{1,5},{6,2},{7,3},{8,12},{9,13},{14,10},{15,11},{16,20},{17,... | collective-permute-start | bytes 1572872 | tf_op jit(solution)/shard_map/ppermute | solution.py:317
  439.5 10.9 %copy-start.16 = (f32[1,256,2048]{2,1,0:T(8,128)S(1)}, f32[1,256,2048]{2,1,0:T(8,128)}, u32[]{:S(2)}) copy-start(f32[1,256,2048]{2,1,0:T(8,128)} %param.15) | copy-start | bytes 6291460
  439.7 10.7 %copy-start.2 = (f32[1,256,2048]{2,1,0:T(8,128)S(1)}, f32[1,256,2048]{2,1,0:T(8,128)}, u32[]{:S(2)}) copy-start(f32[1,256,2048]{2,1,0:T(8,128)} %param.13) | copy-start | bytes 6291460
  (17 other events, 47.2 us)

commit v2 on v1

--- a/solution.py
+++ b/solution.py
@@ -364,9 +364,14 @@
     ]
     base_first = len(table)
     for part in range(2):
-        for s in range(half):
-            table += [(turn - s) % half + core * half, (turn - s) % half + (1 - core) * half]
-    table += [chip ^ r for part in range(2) for r in every] + [home]
+        for other in (core, 1 - core):
+            table += [(turn - s) % half + other * half for s in range(half)]
+    for order in orders:
+        held = [0]
+        for bit in order:
+            held = held + [r ^ bit for r in held]
+        table += [chip ^ r for r in held]
+    table.append(home)
     base_second = len(table)
     table += [0, 0, 0]
     places = jnp.stack([jnp.asarray(value).astype(jnp.int32) for value in table])
@@ -395,65 +400,64 @@
         jnp.concatenate([own_two, other_two], axis=0),
         jnp.concatenate([other_two, own_two], axis=0),
     )
-    pair_two = [pair_two[:, :cols], pair_two[:, cols:]]
-
-    def far_two(part, *others):
-        return send(after(pair_two[part], *others), lambda c, b, h, q: (c, b, 1 - h, q) if b == h else None)
-
-    def spread(held, bit, here):
-        return held | {
-            r ^ bit: send(value, lambda c, b, h, q: (c ^ bit, b, h, q) if (b == h) == here else None)
-            for r, value in sorted(held.items())
-        }
-
-    def rest(held, here):
-        for n in range(1, len(bits)):
-            held = [spread(held[part], orders[part][n], here) for part in range(2)]
-        return held
-
-    def values(held):
-        return [value for part in held for value in part.values()]
-
-    ones = [own_one[:, :cols], own_one[:, cols:]]
-
-    def shift(value, here):
+
+    def to_chips(value, bit, here):
+        return send(value, lambda c, b, h, q: (c ^ bit, b, h, q) if (b == h) == here else None)
+
+    def to_half(value, here):
         if half == 1:
             return jnp.zeros_like(value)
         return send(value, lambda c, b, h, q: (c, b, h, (q + 1) % half) if (b == h) == here else None)
 
-    def far_one(part, *others):
-        return send(
-            after(ones[part], *others), lambda c, b, h, q: (c, 1 - b, 1 - h, q) if b != h else None
-        )
-
+    def begin(pair, here):
+        own = [pair[:, part * cols : (part + 1) * cols] for part in range(2)]
+        return [(value, to_chips(value, order[0], here)) for value, order in zip(own, orders)]
+
+    def proceed(held, here):
+        for n in range(1, len(bits)):
+            held = [jnp.concatenate(pieces, axis=0) for pieces in held]
+            held = [(value, to_chips(value, order[n], here)) for value, order in zip(held, orders)]
+        return held
+
+    def barrier(*values):
+        return jax.tree.unflatten(jax.tree.structure(values), lax.optimization_barrier(jax.tree.leaves(values)))
+
+    ones = [own_one[:, :cols], own_one[:, cols:]]
+
+    def far_half(value):
+        return send(value, lambda c, b, h, q: (c, 1 - b, 1 - h, q) if b != h else None)
+
+    fars, nears = [far_half(ones[0])], [to_half(ones[0], True)]
+    home_two = begin(pair_two, True)
+    ones, fars, nears, pair_two, places, weights, sent = barrier(
+        ones, fars, nears, pair_two, places, weights, sent
+    )
+    far_two = send(pair_two, lambda c, b, h, q: (c, b, 1 - h, q) if b == h else None)
+    turns = [to_half(fars[0], False)]
+    home_two = proceed(home_two, True)
+    ones, fars, nears, turns, far_two, home_two, sent = barrier(ones, fars, nears, turns, far_two, home_two, sent)
+    fars.append(far_half(ones[1]))
+    nears.append(to_half(ones[1], True))
+    away_two = begin(far_two, False)
+    fars, nears, away_two, sent = barrier(fars, nears, away_two, sent)
     got_a = exchange(sent[0])
-    shift_a = shift(ones[0], True)
-    shift_b = shift(ones[1], True)
-    home_two = [spread({0: pair_two[part]}, orders[part][0], True) for part in range(2)]
-    home_two = rest(home_two, True)
-    far_a = far_two(0)
-    far_b = far_two(1)
-    first = (got_a, shift_a, shift_b, far_a, far_b, *values(home_two))
-    away_two = [spread({0: far}, orders[part][0], False) for part, far in enumerate((far_a, far_b))]
-    one_a = far_one(0, *first)
-    one_b = far_one(1, one_a, *values(away_two), places, weights, *sent[1:])
-    turn_a = shift(one_a, False)
-    away_two = rest(away_two, False)
-    turn_b = shift(after(one_b, turn_a, *values(away_two)), False)
+    turns.append(to_half(fars[1], False))
+    away_two = proceed(away_two, False)
     one = []
-    for part, (own, far, near, turned) in enumerate(
-        ((ones[0], one_a, shift_a, turn_a), (ones[1], one_b, shift_b, turn_b))
-    ):
-        first = jnp.where(home, own, far)
-        held = [first]
+    for part in range(2):
+        held = [jnp.where(home, ones[part], fars[part])]
         if half > 1:
-            held.append(jnp.where(home, near, turned))
-        held += [to_turn(first, s) for s in range(2, half)]
-        for value in held:
-            one.append(((value,), part * cols))
-            one.append(((to_core(value),), part * cols))
-    two = [((home_two[part][r], away_two[part][r]), part * cols) for part in range(2) for r in every]
-    got_b = exchange(after(sent[1], got_a, *[p[0][0] for p in one + two]))
+            held.append(jnp.where(home, nears[part], turns[part]))
+        held += [to_turn(held[0], s) for s in range(2, half)]
+        joined = jnp.concatenate(held, axis=0)
+        for value in (joined, to_core(joined)):
+            one += [((value,), part * cols, s * tall_one, tall_one) for s in range(half)]
+    two = []
+    for part in range(2):
+        for mine, theirs in zip(home_two[part], away_two[part]):
+            count = mine.shape[0] // tall_two
+            two += [((mine, theirs), part * cols, n * tall_two, tall_two) for n in range(count)]
+    got_b = exchange(after(sent[1], got_a, away_two[0][1], away_two[1][1]))
     left_a, right_a, start = step(got_a, one, two, rows_dev, True, places, base_first)
     moved = update(left_a, right_a, start, guard)
     left_b, right_b = step(got_b, [((moved,), 0, 0, width)], [((moved,), 0, width, width)], rows_dev, False, places, base_second)
@@ -472,39 +476,42 @@
     def along(both, sums):
         return [*both[0], *[to_turn(value, s) for s, value in enumerate(sums, 1)]]
 
-    def to_owner(terms):
-        return send(summed(*terms).astype(bf16), lambda c, b, h, q: (c, 1 - b, 1 - h, q) if b != h else None)
-
-    def chip_sum(part, here, there, *others):
-        order = orders[part]
-        there = to_chip(there, order[0])
-        held = {}
-        for n, r in enumerate(r for r in every if not r & order[0]):
-            cut = slice(n * tall_two, (n + 1) * tall_two)
-            held[r] = [here[cut], there[cut]]
-        for bit in order[1:]:
+    def to_owner(terms, *others):
+        return send(
+            after(summed(*terms).astype(bf16), *others),
+            lambda c, b, h, q: (c, 1 - b, 1 - h, q) if b != h else None,
+        )
+
+    def chip_sum(part, here, there):
+        there = to_chip(there, orders[part][0])
+        cuts = [slice(n * tall_two, (n + 1) * tall_two) for n in range(chips // 2)]
+        left = [r for r in every if not r & orders[part][0]]
+        return {r: [here[cut], there[cut]] for r, cut in zip(left, cuts)}
+
+    def chip_rest(part, held, *others):
+        held = {r: list(pieces) for r, pieces in held.items()}
+        for bit in orders[part][1:]:
             for r in [r for r in sorted(held) if r & bit]:
                 held[r ^ bit].append(to_chip(after(summed(*held.pop(r)).astype(bf16), *others), bit))
         return held[0]
 
-    def half_sum(parts, firsts, *others):
+    def half_sum(terms, *others):
+        total = summed(*terms)
+        up, down = total[: tall_two // 2], total[tall_two // 2 :]
+        near = send(
+            jnp.where(core == 0, down, up).astype(bf16),
+            lambda c, b, h, q: (c, 1 - b, h, q) if b == h else None,
+        )
         fars = [
             send(
-                after(summed(*terms).astype(bf16), first),
-                lambda c, b, h, q: (c, b, 1 - h, q) if b != h else None,
+                after(rows.astype(bf16), *others),
+                lambda c, b, h, q, to=to: (c, to, 1 - h, q) if b != h else None,
             )
-            for terms, first in zip(parts, firsts)
+            for to, rows in enumerate((up, down))
         ]
-        sums = []
-        for terms, far in zip(parts, fars):
-            total = summed(*terms, far)
-            up, down = total[: tall_two // 2], total[tall_two // 2 :]
-            passed = send(
-                after(jnp.where(core == 0, down, up).astype(bf16), *others),
-                lambda c, b, h, q: (c, 1 - b, h, q) if b == h else None,
-            )
-            sums.append(jnp.where(home, jnp.where(core == 0, up, down), passed.astype(f32)))
-        return sums
+        return jnp.where(home, jnp.where(core == 0, up, down), near.astype(f32)) + jnp.where(
+            core == 0, *[far.astype(f32) for far in fars]
+        )
 
     def outer(module, moment, sums):
         average = jnp.concatenate(sums, axis=1)[None]
@@ -518,15 +525,16 @@
     leave_a, leave_b = deltas(calls[2], here_a, *sums_a, *sums_b)
     along_a, along_b = along(both_a, sums_a), along(both_b, sums_b)
     stay_a, stay_b = deltas(calls[3], leave_a, along_a[-1])
-    owned_a, owned_b = to_owner(along_a), to_owner(along_b)
+    owned_a = to_owner(along_a)
+    owned_b = to_owner(along_b, stay_a)
+    chip_a, chip_b = chip_sum(0, stay_a, leave_a), chip_sum(1, stay_b, leave_b)
+    chip_a, chip_b = chip_rest(0, chip_a, owned_a), chip_rest(1, chip_b, owned_a)
     sums_one = [
         jnp.where(home, summed(*terms), owned.astype(f32))
         for terms, owned in ((along_a, owned_a), (along_b, owned_b))
     ]
     new_one, next_moment_one = outer(module_one, moment_one, sums_one)
-    chip_a = chip_sum(0, stay_a, leave_a, owned_a)
-    chip_b = chip_sum(1, stay_b, leave_b, owned_a)
-    sums_two = half_sum((chip_a, chip_b), (owned_b, owned_b), new_one, next_moment_one)
+    sums_two = [half_sum(terms, owned_b) for terms in (chip_a, chip_b)]
     new_two, next_moment_two = outer(module_two, moment_two, sums_two)
     return (new_one, new_two, next_moment_one, next_moment_two)
 

time: 455 us -> 417 us (0.916)
  waiting for transfers between devices: 217 us -> 175 us
    ppermute x39 -> x34, waiting for transfers between devices: 204 us -> 162 us  [send(): return lax.ppermute(value, ('row', 'col'), pairs)]
    convert_element_type x4 -> x2, other arithmetic: 10.1 us -> 3.26 us  [chip_rest(): summed(*held.pop(r)).astype(bf16)]
    concatenate x0 -> x4, other arithmetic: none -> 4.67 us  [the longest x2 3.01 us: proceed(): held = [jnp.concatenate(pieces, axis=0) for pieces in held]]
    ppermute x39 -> x34, starting transfers between devices: 62.2 us -> 62.7 us  [send(): return lax.ppermute(value, ('row', 'col'), pairs)]
  transfers between devices with their start and end apart: 41 -> 36, of which waited for: 16 -> 11; matrix products, arithmetic and copies ran while one was open for 11% -> 14% of each run, Pallas kernels for 15% -> 16%
where the time goes in v2:
time: 417 us; the launch traced here: 415 us
  waiting for transfers between devices  175 us (42%)
  Pallas kernels  94.3 us (23%)
  starting transfers between devices  71.1 us (17%)
  other arithmetic  53.4 us (13%)
  local copies, waits for them, and re-layouts  11.5 us (3%)
  matrix products  5.46 us (1%)
    ppermute x34, waiting for transfers between devices, send(): return lax.ppermute(value, ('row', 'col'), pairs)  162 us
    ppermute x34, starting transfers between devices, send(): return lax.ppermute(value, ('row', 'col'), pairs)  62.7 us
    pallas_call x4, Pallas kernels, terms(): pl.pallas_call(functools.partial(term_kernel, guard * width ** 0.5, 256,...  44 us
    pallas_call x2, Pallas kernels, step(): pl.pallas_call(functools.partial(step_kernel, rows_dev, tile, keep, base,...  31.6 us
    pallas_call x1, Pallas kernels, update(): pl.pallas_call(functools.partial(update_kernel, guard * width ** 0.5, 512...  18.8 us
    all_to_all x2, waiting for transfers between devices, exchange(): lax.all_to_all(value.reshape(paths, room, 2 * width), ('row', 'col'), spl...  13 us
    sub x2, other arithmetic, outer(): module - outer_rate * (outer_moment * following + average)  11.5 us
    all_to_all x2, starting transfers between devices, exchange(): lax.all_to_all(value.reshape(paths, room, 2 * width), ('row', 'col'), spl...  8.48 us
  transfers between devices with their start and end apart: 36, of which 11 were waited for; matrix products, arithmetic and copies ran while one was open for 14% of the time, Pallas kernels for 16%

profile of v2, /device:TPU:1, one launch (start us, length us, event | category | flops | bytes accessed | tf_op | source)
XLA Modules:
  0.0 415.4 jit_solution(156726872188367391)
XLA Ops:
  0.6 2.5 convert_bitcast_fusion
  3.1 1.5 fusion.22
  4.7 1.8 collective-permute-start.1
  6.5 5.6 %collective-permute-start = (bf16[512,1024]{1,0:T(8,128)(2,1)}, bf16[512,1024]{1,0:T(8,128)(2,1)}, u32[]{:S(2)}, u32[]{:S(2)}) collective-permute-start(bf16[512,1024]{1,0:T(8,128)(2,1)} %get-tuple-element.75), channel_id=1, source_target_pairs={{2,4},{3,5},{4,2},{5,3},{10,12},{11,13},{12,10},{13,11},{18,20},{1... | collective-permute-start | bytes 3145736 | tf_op jit(solution)/shard_map/ppermute | solution.py:317
  12.2 2.3 collective-permute-start.2
  17.2 2.5 maximum_select_fusion
  21.0 1.6 collective-permute-start.5
  28.4 3.3 convolution_convert_fusion
  31.8 2.1 convolution_convert_fusion.1
  33.9 2.2 collective-permute-done
  37.4 1.4 pad_maximum_fusion.refs_10_.refs_12_
  39.8 1.6 pad_maximum_fusion.1.refs_18_.refs_20_
  42.2 2.4 collective-permute-start.3
  44.6 23.3 %collective-permute-done.3 = bf16[512,1024]{1,0:T(8,128)(2,1)S(1)} collective-permute-done((bf16[512,1024]{1,0:T(8,128)(2,1)}, bf16[512,1024]{1,0:T(8,128)(2,1)S(1)}, u32[]{:S(2)}, u32[]{:S(2)}) %collective-permute-start.3) | collective-permute-done | bytes 1048608 | tf_op jit(solution)/shard_map/ppermute | solution.py:317
  68.0 18.3 %collective-permute-done.4 = bf16[512,2048]{1,0:T(8,128)(2,1)S(1)} collective-permute-done((bf16[512,2048]{1,0:T(8,128)(2,1)S(1)}, bf16[512,2048]{1,0:T(8,128)(2,1)S(1)}, u32[]{:S(2)}, u32[]{:S(2)}) %collective-permute-start.4) | collective-permute-done | bytes 2097184 | tf_op jit(solution)/shard_map/ppermute | solution.py:317
  87.7 1.9 collective-permute-start.9
  89.8 3.1 collective-permute-start.12
  93.0 3.1 collective-permute-start.11
  96.1 19.8 %collective-permute-done.9 = bf16[512,1024]{1,0:T(8,128)(2,1)S(1)} collective-permute-done((bf16[512,1024]{1,0:T(8,128)(2,1)S(1)}, bf16[512,1024]{1,0:T(8,128)(2,1)S(1)}, u32[]{:S(2)}, u32[]{:S(2)}) %collective-permute-start.9) | collective-permute-done | bytes 1048608 | tf_op jit(solution)/shard_map/ppermute | solution.py:317
  118.2 4.2 %all-to-all-start = ((bf16[32,8,4096]{2,1,0:T(8,128)(2,1)}), bf16[32,8,4096]{2,1,0:T(8,128)(2,1)}, u32[]{:S(2)}, u32[]{:S(2)}) async-start(bf16[32,8,4096]{2,1,0:T(8,128)(2,1)} %bitcast.73), calls=%async_computation | async-start | bytes 4194304 | tf_op jit(solution)/shard_map/all_to_all | solution.py:391
  122.5 3.4 collective-permute-start.14
  126.2 3.4 collective-permute-start.17
  129.6 3.1 collective-permute-start.16
  132.7 1.6 broadcast_select_fusion.2
  136.0 34.9 %collective-permute-done.14 = bf16[512,1024]{1,0:T(8,128)(2,1)S(1)} collective-permute-done((bf16[512,1024]{1,0:T(8,128)(2,1)}, bf16[512,1024]{1,0:T(8,128)(2,1)S(1)}, u32[]{:S(2)}, u32[]{:S(2)}) %collective-permute-start.14) | collective-permute-done | bytes 1048608 | tf_op jit(solution)/shard_map/ppermute | solution.py:317
  171.0 1.5 pad_maximum_fusion.3.refs_6_.refs_7_
  172.5 1.3 copy-done.32
  173.9 4.3 %all-to-all-start.1 = ((bf16[32,8,4096]{2,1,0:T(8,128)(2,1)}), bf16[32,8,4096]{2,1,0:T(8,128)(2,1)}, u32[]{:S(2)}, u32[]{:S(2)}) async-start(bf16[32,8,4096]{2,1,0:T(8,128)(2,1)} %bitcast.27), calls=%async_computation.1 | async-start | bytes 4194304 | tf_op jit(solution)/shard_map/all_to_all | solution.py:391
  178.2 16.5 %shard_map.111 = (bf16[256,4096]{1,0:T(8,128)(2,1)}, bf16[256,4096]{1,0:T(8,128)(2,1)}, bf16[4096,2048]{1,0:T(8,128)(2,1)}) custom-call(s32[84]{0:T(128)} %stack.94.refs_0_.place_ref, bf16[256,4096]{1,0:T(8,128)(2,1)} %bitcast.26.refs_1_, bf16[1024,1024]{1,0:T(8,128)(2,1)} %copy-done.11, bf16[1024,1024]{1,0:T(8,128)(2,1)} %copy-done.11, ...), custom_call_target="tpu_custom_call" | custom-call | flops 16106127360 | bytes 16777216 | tf_op jit(solution)/shard_map/pallas_call | solution.py:142
  194.7 18.8 %shard_map.112.refs_2_.refs_3_ = bf16[4096,2048]{1,0:T(8,128)(2,1)} custom-call(bf16[256,4096]{1,0:T(8,128)(2,1)} %get-tuple-element.89.a_ref, bf16[256,4096]{1,0:T(8,128)(2,1)} %get-tuple-element.90.b_ref, bf16[4096,2048]{1,0:T(8,128)(2,1)} %get-tuple-element.93.p_ref), custom_call_target="tpu_custom_call" | custom-call | flops 25769803776 | bytes 33554432 | tf_op jit(solution)/shard_map/pallas_call | solution.py:176
  213.4 13.0 %all-to-all-done.1 = bf16[32,8,4096]{2,1,0:T(8,128)(2,1)} async-done(((bf16[32,8,4096]{2,1,0:T(8,128)(2,1)}), bf16[32,8,4096]{2,1,0:T(8,128)(2,1)}, u32[]{:S(2)}, u32[]{:S(2)}) %all-to-all-start.1) | async-done | bytes 2097184 | tf_op jit(solution)/shard_map/all_to_all | solution.py:391
  226.4 15.1 %shard_map.113 = (bf16[256,4096]{1,0:T(8,128)(2,1)}, bf16[256,4096]{1,0:T(8,128)(2,1)}) custom-call(s32[84]{0:T(128)} %stack.94.refs_0_.place_ref, bf16[256,4096]{1,0:T(8,128)(2,1)} %bitcast.28.refs_1_, bf16[4096,2048]{1,0:T(8,128)(2,1)} %shard_map.112.refs_2_.refs_3_, bf16[4096,2048]{1,0:T(8,128)(2,1)} %shard_map.112.refs_2_.refs_3_), custom_call_target="tpu_custom_call" | custom-call | flops 16106127360 | bytes 16777216 | tf_op jit(solution)/shard_map/pallas_call | solution.py:142
  241.5 11.0 %shard_map.114 = (bf16[1024,1024]{1,0:T(8,128)(2,1)}, bf16[1024,1024]{1,0:T(8,128)(2,1)}) custom-call(s32[84]{0:T(128)} %stack.94.refs_0_.place_ref, f32[2]{0:T(128)} %pad_maximum_fusion.4.weight_ref, bf16[256,4096]{1,0:T(8,128)(2,1)} %get-tuple-element.89.a_ref, bf16[256,4096]{1,0:T(8,128)(2,1)} %get-tuple-element.90.b_ref, ...), custom_call_target="tpu_custom_call" | custom-call | flops 1 | bytes 1 | tf_op jit(solution)/shard_map/pallas_call | solution.py:255
  253.1 11.0 %shard_map.115 = (bf16[1024,1024]{1,0:T(8,128)(2,1)}, bf16[1024,1024]{1,0:T(8,128)(2,1)}) custom-call(s32[84]{0:T(128)} %stack.94.refs_0_.place_ref, f32[2]{0:T(128)} %pad_maximum_fusion.4.weight_ref, bf16[256,4096]{1,0:T(8,128)(2,1)} %get-tuple-element.89.a_ref, bf16[256,4096]{1,0:T(8,128)(2,1)} %get-tuple-element.90.b_ref, ...), custom_call_target="tpu_custom_call" | custom-call | flops 1 | bytes 1 | tf_op jit(solution)/shard_map/pallas_call | solution.py:255
  264.1 2.7 add_convert_fusion.3
  266.8 1.9 collective-permute-start.19
  268.8 1.4 add_convert_fusion.2
  270.1 11.0 %shard_map.116 = (bf16[1024,1024]{1,0:T(8,128)(2,1)}, bf16[1024,1024]{1,0:T(8,128)(2,1)}) custom-call(s32[84]{0:T(128)} %stack.94.refs_0_.place_ref, f32[2]{0:T(128)} %pad_maximum_fusion.4.weight_ref, bf16[256,4096]{1,0:T(8,128)(2,1)} %get-tuple-element.89.a_ref, bf16[256,4096]{1,0:T(8,128)(2,1)} %get-tuple-element.90.b_ref, ...), custom_call_target="tpu_custom_call" | custom-call | flops 1 | bytes 1 | tf_op jit(solution)/shard_map/pallas_call | solution.py:255
  282.9 9.3 %collective-permute-done.19 = bf16[512,1024]{1,0:T(8,128)(2,1)S(1)} collective-permute-done((bf16[512,1024]{1,0:T(8,128)(2,1)}, bf16[512,1024]{1,0:T(8,128)(2,1)S(1)}, u32[]{:S(2)}, u32[]{:S(2)}) %collective-permute-start.19) | collective-permute-done | bytes 1048608 | tf_op jit(solution)/shard_map/ppermute | solution.py:317
  292.2 2.8 fusion
  295.1 4.0 collective-permute-start.20
  299.0 11.0 %shard_map.117 = (bf16[1024,1024]{1,0:T(8,128)(2,1)}, bf16[1024,1024]{1,0:T(8,128)(2,1)}) custom-call(s32[84]{0:T(128)} %stack.94.refs_0_.place_ref, f32[2]{0:T(128)} %pad_maximum_fusion.4.weight_ref, bf16[256,4096]{1,0:T(8,128)(2,1)} %get-tuple-element.89.a_ref, bf16[256,4096]{1,0:T(8,128)(2,1)} %get-tuple-element.90.b_ref, ...), custom_call_target="tpu_custom_call" | custom-call | flops 1 | bytes 1 | tf_op jit(solution)/shard_map/pallas_call | solution.py:255
  310.1 15.9 %collective-permute-done.22 = bf16[512,1024]{1,0:T(8,128)(2,1)} collective-permute-done((bf16[512,1024]{1,0:T(8,128)(2,1)}, bf16[512,1024]{1,0:T(8,128)(2,1)}, u32[]{:S(2)}, u32[]{:S(2)}) %collective-permute-start.22) | collective-permute-done | bytes 1048608 | tf_op jit(solution)/shard_map/ppermute | solution.py:317
  325.9 1.8 fusion.1
  327.8 2.1 collective-permute-start.23
  329.9 1.6 add_convert_fusion
  331.5 1.6 collective-permute-start.30
  333.1 1.6 add_convert_fusion.1
  335.1 3.4 convert_select_fusion.1
  338.4 16.9 %collective-permute-done.23 = bf16[512,1024]{1,0:T(8,128)(2,1)S(1)} collective-permute-done((bf16[512,1024]{1,0:T(8,128)(2,1)S(1)}, bf16[512,1024]{1,0:T(8,128)(2,1)S(1)}, u32[]{:S(2)}, u32[]{:S(2)}) %collective-permute-start.23) | collective-permute-done | bytes 1048608 | tf_op jit(solution)/shard_map/ppermute | solution.py:317
  355.3 3.4 convert_select_fusion
  358.7 1.8 convert_add_fusion
  361.7 1.8 collective-permute-start.32
  363.4 1.9 collective-permute-start.33
  366.7 2.0 convert_add_fusion.1
  369.9 5.4 %collective-permute-start.27 = (bf16[256,1024]{1,0:T(8,128)(2,1)}, bf16[256,1024]{1,0:T(8,128)(2,1)}, u32[]{:S(2)}, u32[]{:S(2)}) collective-permute-start(bf16[256,1024]{1,0:T(8,128)(2,1)} %get-tuple-element.107), channel_id=1, source_target_pairs={{2,0},{3,1},{4,2},{5,3},{10,8},{11,9},{12,10},{13,11},{18,16},{19,... | collective-permute-start | bytes 1572872 | tf_op jit(solution)/shard_map/ppermute | solution.py:317
  375.3 2.2 collective-permute-start.28
  377.4 1.6 collective-permute-start.26
  379.0 8.8 %multiply_subtract_fusion = (f32[1,512,2048]{2,1,0:T(8,128)}, f32[1,512,2048]{2,1,0:T(8,128)}) fusion(f32[1,512,2048]{2,1,0:T(8,128)S(1)} %copy-done, f32[512,1024]{1,0:T(8,128)} %convert_select_fusion, f32[512,1024]{1,0:T(8,128)} %convert_select_fusion.1, f32[1,512,2048]{2,1,0:T(8,128)} %param.14), kind=kLoop, calls=%fused_computation.3 | loop fusion | flops 7340032 | bytes 20971520 | tf_op jit(solution)/shard_map/sub | solution.py:519
  387.8 11.7 %collective-permute-done.33 = bf16[256,1024]{1,0:T(8,128)(2,1)S(1)} collective-permute-done((bf16[256,1024]{1,0:T(8,128)(2,1)}, bf16[256,1024]{1,0:T(8,128)(2,1)S(1)}, u32[]{:S(2)}, u32[]{:S(2)}) %collective-permute-start.33) | collective-permute-done | bytes 524320 | tf_op jit(solution)/shard_map/ppermute | solution.py:317
  399.5 1.4 select_add_fusion
  401.0 9.9 %collective-permute-done.28 = bf16[256,1024]{1,0:T(8,128)(2,1)} collective-permute-done((bf16[256,1024]{1,0:T(8,128)(2,1)}, bf16[256,1024]{1,0:T(8,128)(2,1)}, u32[]{:S(2)}, u32[]{:S(2)}) %collective-permute-start.28) | collective-permute-done | bytes 524320 | tf_op jit(solution)/shard_map/ppermute | solution.py:317
  410.9 1.8 select_add_fusion.1
  412.7 2.7 multiply_subtract_fusion.1
  (138 shorter events, 22.5 us)
Async XLA Ops:
  3.1 8.9 %copy-start.1 = (f32[1,256,2048]{2,1,0:T(8,128)S(1)}, f32[1,256,2048]{2,1,0:T(8,128)}, u32[]{:S(2)}) copy-start(f32[1,256,2048]{2,1,0:T(8,128)} %param.13) | copy-start | bytes 6291460
  4.7 9.9 %copy-start.29 = (s32[2,128,1]{1,2,0:T(1,128)S(1)}, s32[2,128,1]{1,2,0:T(1,128)}, u32[]{:S(2)}) copy-start(s32[2,128,1]{1,2,0:T(1,128)} %param.10) | copy-start | bytes 3076
  4.7 10.5 %copy-start.16 = (bf16[2,128,2048]{2,1,0:T(8,128)(2,1)S(1)}, bf16[2,128,2048]{2,1,0:T(8,128)(2,1)}, u32[]{:S(2)}) copy-start(bf16[2,128,2048]{2,1,0:T(8,128)(2,1)} %param.8) | copy-start | bytes 3145732
  4.7 11.5 %copy-start.17 = (bf16[2,128,2048]{2,1,0:T(8,128)(2,1)S(1)}, bf16[2,128,2048]{2,1,0:T(8,128)(2,1)}, u32[]{:S(2)}) copy-start(bf16[2,128,2048]{2,1,0:T(8,128)(2,1)} %param.9) | copy-start | bytes 3145732
  4.7 29.2 %collective-permute-start.1 = (bf16[512,1024]{1,0:T(8,128)(2,1)}, bf16[512,1024]{1,0:T(8,128)(2,1)}, u32[]{:S(2)}, u32[]{:S(2)}) collective-permute-start(bf16[512,1024]{1,0:T(8,128)(2,1)} %get-tuple-element.75), channel_id=1, source_target_pairs={{0,1},{1,0},{6,7},{7,6},{8,9},{9,8},{14,15},{15,14},{16,17},{17,16... | collective-permute-start | bytes 3145736 | tf_op jit(solution)/shard_map/ppermute | solution.py:317
  6.5 29.7 %collective-permute-start = (bf16[512,1024]{1,0:T(8,128)(2,1)}, bf16[512,1024]{1,0:T(8,128)(2,1)}, u32[]{:S(2)}, u32[]{:S(2)}) collective-permute-start(bf16[512,1024]{1,0:T(8,128)(2,1)} %get-tuple-element.75), channel_id=1, source_target_pairs={{2,4},{3,5},{4,2},{5,3},{10,12},{11,13},{12,10},{13,11},{18,20},{1... | collective-permute-start | bytes 3145736 | tf_op jit(solution)/shard_map/ppermute | solution.py:317
  12.2 5.0 %collective-permute-start.2 = (bf16[256,2048]{1,0:T(8,128)(2,1)S(1)}, bf16[256,2048]{1,0:T(8,128)(2,1)}, u32[]{:S(2)}, u32[]{:S(2)}) collective-permute-start(bf16[256,2048]{1,0:T(8,128)(2,1)S(1)} %convert_bitcast_fusion.1), channel_id=1, source_target_pairs={{2,6},{3,7},{4,0},{5,1},{10,14},{11,15},{12,8},{13,9},{18,22},{19,... | collective-permute-start | bytes 3145736 | tf_op jit(solution)/shard_map/ppermute | solution.py:317
  19.8 2.9 copy-start.28
  21.0 16.4 %collective-permute-start.5 = (bf16[512,1024]{1,0:T(8,128)(2,1)S(1)}, bf16[512,1024]{1,0:T(8,128)(2,1)}, u32[]{:S(2)}, u32[]{:S(2)}) collective-permute-start(bf16[512,1024]{1,0:T(8,128)(2,1)S(1)} %get-tuple-element.130), channel_id=1, source_target_pairs={{0,8},{1,9},{6,14},{7,15},{8,0},{9,1},{14,6},{15,7},{16,24},{17,25... | collective-permute-start | bytes 3145736 | tf_op jit(solution)/shard_map/ppermute | solution.py:317
  26.8 4.9 %copy-start.12 = (bf16[128,2048]{1,0:T(8,128)(2,1)S(1)}, bf16[128,2048]{1,0:T(8,128)(2,1)}, u32[]{:S(2)}) copy-start(bf16[128,2048]{1,0:T(8,128)(2,1)} %get-tuple-element.134) | copy-start | bytes 1572868
  26.8 4.9 %copy-start.13 = (bf16[128,2048]{1,0:T(8,128)(2,1)S(1)}, bf16[128,2048]{1,0:T(8,128)(2,1)}, u32[]{:S(2)}) copy-start(bf16[128,2048]{1,0:T(8,128)(2,1)} %get-tuple-element.136) | copy-start | bytes 1572868
  27.0 12.8 %collective-permute-start.7 = (bf16[512,1024]{1,0:T(8,128)(2,1)}, bf16[512,1024]{1,0:T(8,128)(2,1)S(1)}, u32[]{:S(2)}, u32[]{:S(2)}) collective-permute-start(bf16[512,1024]{1,0:T(8,128)(2,1)} %get-tuple-element.129), channel_id=1, source_target_pairs={{0,16},{1,17},{6,22},{7,23},{8,24},{9,25},{14,30},{15,31},{16,0},{... | collective-permute-start | bytes 3145736 | tf_op jit(solution)/shard_map/ppermute | solution.py:317
  36.1 50.1 %collective-permute-start.4 = (bf16[512,2048]{1,0:T(8,128)(2,1)S(1)}, bf16[512,2048]{1,0:T(8,128)(2,1)S(1)}, u32[]{:S(2)}, u32[]{:S(2)}) collective-permute-start(bf16[512,2048]{1,0:T(8,128)(2,1)S(1)} %maximum_select_fusion), channel_id=1, source_target_pairs={{0,2},{1,3},{6,4},{7,5},{8,10},{9,11},{14,12},{15,13},{16,18},{17,... | collective-permute-start | bytes 6291464 | tf_op jit(solution)/shard_map/ppermute | solution.py:317
  38.8 2.6 copy-start.9
  38.8 47.4 %copy-start.5 = (bf16[512,1024]{1,0:T(8,128)(2,1)S(1)}, bf16[512,1024]{1,0:T(8,128)(2,1)}, u32[]{:S(2)}) copy-start(bf16[512,1024]{1,0:T(8,128)(2,1)} %get-tuple-element.69) | copy-start | bytes 3145732
  38.9 47.4 %collective-permute-start.6 = (bf16[1024,1024]{1,0:T(8,128)(2,1)S(1)}, bf16[1024,1024]{1,0:T(8,128)(2,1)S(1)}, u32[]{:S(2)}, u32[]{:S(2)}) collective-permute-start(bf16[1024,1024]{1,0:T(8,128)(2,1)S(1)} %pad_maximum_fusion.refs_10_.refs_12_), channel_id=1, source_target_pairs={{0,16},{1,17},{6,22},{7,23},{8,24},{9,25},{14,30},{15,31},{16,0},{... | collective-permute-start | bytes 6291464 | tf_op jit(solution)/shard_map/ppermute | solution.py:317
  41.4 48.4 %copy-start.10 = (bf16[1024,1024]{1,0:T(8,128)(2,1)}, bf16[1024,1024]{1,0:T(8,128)(2,1)S(1)}, u32[]{:S(2)}) copy-start(bf16[1024,1024]{1,0:T(8,128)(2,1)S(1)} %pad_maximum_fusion.1.refs_18_.refs_20_) | copy-start | bytes 6291460
  41.4 44.8 %collective-permute-start.8 = (bf16[1024,1024]{1,0:T(8,128)(2,1)S(1)}, bf16[1024,1024]{1,0:T(8,128)(2,1)S(1)}, u32[]{:S(2)}, u32[]{:S(2)}) collective-permute-start(bf16[1024,1024]{1,0:T(8,128)(2,1)S(1)} %pad_maximum_fusion.1.refs_18_.refs_20_), channel_id=1, source_target_pairs={{0,8},{1,9},{6,14},{7,15},{8,0},{9,1},{14,6},{15,7},{16,24},{17,25... | collective-permute-start | bytes 6291464 | tf_op jit(solution)/shard_map/ppermute | solution.py:317
  42.2 25.7 %collective-permute-start.3 = (bf16[512,1024]{1,0:T(8,128)(2,1)}, bf16[512,1024]{1,0:T(8,128)(2,1)S(1)}, u32[]{:S(2)}, u32[]{:S(2)}) collective-permute-start(bf16[512,1024]{1,0:T(8,128)(2,1)} %collective-permute-done), channel_id=1, source_target_pairs={{2,3},{3,2},{4,5},{5,4},{10,11},{11,10},{12,13},{13,12},{18,19},{1... | collective-permute-start | bytes 3145736 | tf_op jit(solution)/shard_map/ppermute | solution.py:317
  68.0 19.1 %copy-start.14 = (bf16[512,1024]{1,0:T(8,128)(2,1)}, bf16[512,1024]{1,0:T(8,128)(2,1)S(1)}, u32[]{:S(2)}) copy-start(bf16[512,1024]{1,0:T(8,128)(2,1)S(1)} %collective-permute-done.3) | copy-start | bytes 3145732
  86.3 3.5 copy-start.30
  86.3 9.8 %collective-permute-start.10 = (bf16[512,1024]{1,0:T(8,128)(2,1)S(1)}, bf16[512,1024]{1,0:T(8,128)(2,1)S(1)}, u32[]{:S(2)}, u32[]{:S(2)}) collective-permute-start(bf16[512,1024]{1,0:T(8,128)(2,1)S(1)} %copy-done.5), channel_id=1, source_target_pairs={{0,1},{1,0},{6,7},{7,6},{8,9},{9,8},{14,15},{15,14},{16,17},{17,16... | collective-permute-start | bytes 3145736 | tf_op jit(solution)/shard_map/ppermute | solution.py:317
  87.7 28.2 %collective-permute-start.9 = (bf16[512,1024]{1,0:T(8,128)(2,1)S(1)}, bf16[512,1024]{1,0:T(8,128)(2,1)S(1)}, u32[]{:S(2)}, u32[]{:S(2)}) collective-permute-start(bf16[512,1024]{1,0:T(8,128)(2,1)S(1)} %copy-done.5), channel_id=1, source_target_pairs={{2,4},{3,5},{4,2},{5,3},{10,12},{11,13},{12,10},{13,11},{18,20},{1... | collective-permute-start | bytes 3145736 | tf_op jit(solution)/shard_map/ppermute | solution.py:317
  89.8 26.1 %collective-permute-start.12 = (bf16[512,1024]{1,0:T(8,128)(2,1)S(1)}, bf16[512,1024]{1,0:T(8,128)(2,1)S(1)}, u32[]{:S(2)}, u32[]{:S(2)}) collective-permute-start(bf16[512,1024]{1,0:T(8,128)(2,1)S(1)} %get-tuple-element.86), channel_id=1, source_target_pairs={{2,18},{3,19},{4,20},{5,21},{10,26},{11,27},{12,28},{13,29},{18,2}... | collective-permute-start | bytes 3145736 | tf_op jit(solution)/shard_map/ppermute | solution.py:317
  93.0 23.0 %collective-permute-start.11 = (bf16[512,1024]{1,0:T(8,128)(2,1)S(1)}, bf16[512,1024]{1,0:T(8,128)(2,1)S(1)}, u32[]{:S(2)}, u32[]{:S(2)}) collective-permute-start(bf16[512,1024]{1,0:T(8,128)(2,1)S(1)} %get-tuple-element.82), channel_id=1, source_target_pairs={{2,10},{3,11},{4,12},{5,13},{10,2},{11,3},{12,4},{13,5},{18,26},{1... | collective-permute-start | bytes 3145736 | tf_op jit(solution)/shard_map/ppermute | solution.py:317
  96.1 19.8 %copy-start.18 = (bf16[512,1024]{1,0:T(8,128)(2,1)}, bf16[512,1024]{1,0:T(8,128)(2,1)S(1)}, u32[]{:S(2)}) copy-start(bf16[512,1024]{1,0:T(8,128)(2,1)S(1)} %collective-permute-done.10) | copy-start | bytes 3145732
  118.2 55.6 %all-to-all-start = ((bf16[32,8,4096]{2,1,0:T(8,128)(2,1)}), bf16[32,8,4096]{2,1,0:T(8,128)(2,1)}, u32[]{:S(2)}, u32[]{:S(2)}) async-start(bf16[32,8,4096]{2,1,0:T(8,128)(2,1)} %bitcast.73), calls=%async_computation | async-start | bytes 4194304 | tf_op jit(solution)/shard_map/all_to_all | solution.py:391
  122.4 3.6 copy-start.25
  122.5 48.4 %collective-permute-start.14 = (bf16[512,1024]{1,0:T(8,128)(2,1)}, bf16[512,1024]{1,0:T(8,128)(2,1)S(1)}, u32[]{:S(2)}, u32[]{:S(2)}) collective-permute-start(bf16[512,1024]{1,0:T(8,128)(2,1)} %copy-done.20), channel_id=1, source_target_pairs={{2,3},{3,2},{4,5},{5,4},{10,11},{11,10},{12,13},{13,12},{18,19},{1... | collective-permute-start | bytes 3145736 | tf_op jit(solution)/shard_map/ppermute | solution.py:317
  126.0 3.6 copy-start.23
  126.1 6.7 %copy-start.15 = (bf16[512,1024]{1,0:T(8,128)(2,1)S(1)}, bf16[512,1024]{1,0:T(8,128)(2,1)}, u32[]{:S(2)}) copy-start(bf16[512,1024]{1,0:T(8,128)(2,1)} %copy-done.14) | copy-start | bytes 3145732
  126.2 8.2 %copy-start.27 = (bf16[1024,1024]{1,0:T(8,128)(2,1)}, bf16[1024,1024]{1,0:T(8,128)(2,1)S(1)}, u32[]{:S(2)}) copy-start(bf16[1024,1024]{1,0:T(8,128)(2,1)S(1)} %constant_dynamic-update-slice_fusion.2.refs_19_.refs_21_) | copy-start | bytes 6291460
  126.2 46.4 %collective-permute-start.17 = (bf16[1024,1024]{1,0:T(8,128)(2,1)S(1)}, bf16[1024,1024]{1,0:T(8,128)(2,1)S(1)}, u32[]{:S(2)}, u32[]{:S(2)}) collective-permute-start(bf16[1024,1024]{1,0:T(8,128)(2,1)S(1)} %constant_dynamic-update-slice_fusion.2.refs_19_.refs_21_), channel_id=1, source_target_pairs={{2,10},{3,11},{4,12},{5,13},{10,2},{11,3},{12,4},{13,5},{18,26},{1... | collective-permute-start | bytes 6291464 | tf_op jit(solution)/shard_map/ppermute | solution.py:317
  129.6 4.7 %copy-start.26 = (bf16[1024,1024]{1,0:T(8,128)(2,1)}, bf16[1024,1024]{1,0:T(8,128)(2,1)S(1)}, u32[]{:S(2)}) copy-start(bf16[1024,1024]{1,0:T(8,128)(2,1)S(1)} %constant_dynamic-update-slice_fusion.refs_11_.refs_13_) | copy-start | bytes 6291460
  129.6 44.2 %collective-permute-start.16 = (bf16[1024,1024]{1,0:T(8,128)(2,1)S(1)}, bf16[1024,1024]{1,0:T(8,128)(2,1)}, u32[]{:S(2)}, u32[]{:S(2)}) collective-permute-start(bf16[1024,1024]{1,0:T(8,128)(2,1)S(1)} %constant_dynamic-update-slice_fusion.refs_11_.refs_13_), channel_id=1, source_target_pairs={{2,18},{3,19},{4,20},{5,21},{10,26},{11,27},{12,28},{13,29},{18,2}... | collective-permute-start | bytes 6291464 | tf_op jit(solution)/shard_map/ppermute | solution.py:317
  134.3 1.5 copy-start.21
  134.5 36.5 %copy-start.11 = (bf16[1024,1024]{1,0:T(8,128)(2,1)}, bf16[1024,1024]{1,0:T(8,128)(2,1)S(1)}, u32[]{:S(2)}) copy-start(bf16[1024,1024]{1,0:T(8,128)(2,1)S(1)} %pad_maximum_fusion.2.refs_2_.refs_3_) | copy-start | bytes 6291460
  134.5 36.3 %copy-start.19 = (bf16[512,1024]{1,0:T(8,128)(2,1)S(1)}, bf16[512,1024]{1,0:T(8,128)(2,1)}, u32[]{:S(2)}) copy-start(bf16[512,1024]{1,0:T(8,128)(2,1)} %copy-done.18) | copy-start | bytes 3145732
  134.5 43.6 %collective-permute-start.13 = (bf16[1024,1024]{1,0:T(8,128)(2,1)S(1)}, bf16[1024,1024]{1,0:T(8,128)(2,1)}, u32[]{:S(2)}, u32[]{:S(2)}) collective-permute-start(bf16[1024,1024]{1,0:T(8,128)(2,1)S(1)} %pad_maximum_fusion.2.refs_2_.refs_3_), channel_id=1, source_target_pairs={{0,4},{1,5},{2,6},{3,7},{4,0},{5,1},{6,2},{7,3},{8,12},{9,13},{10,... | collective-permute-start | bytes 6291464 | tf_op jit(solution)/shard_map/ppermute | solution.py:317
  172.5 5.6 %collective-permute-start.15 = (bf16[1024,1024]{1,0:T(8,128)(2,1)}, bf16[1024,1024]{1,0:T(8,128)(2,1)}, u32[]{:S(2)}, u32[]{:S(2)}) collective-permute-start(bf16[1024,1024]{1,0:T(8,128)(2,1)} %pad_maximum_fusion.3.refs_6_.refs_7_), channel_id=1, source_target_pairs={{0,4},{1,5},{2,6},{3,7},{4,0},{5,1},{6,2},{7,3},{8,12},{9,13},{10,... | collective-permute-start | bytes 6291464 | tf_op jit(solution)/shard_map/ppermute | solution.py:317
  173.9 52.6 %all-to-all-start.1 = ((bf16[32,8,4096]{2,1,0:T(8,128)(2,1)}), bf16[32,8,4096]{2,1,0:T(8,128)(2,1)}, u32[]{:S(2)}, u32[]{:S(2)}) async-start(bf16[32,8,4096]{2,1,0:T(8,128)(2,1)} %bitcast.27), calls=%async_computation.1 | async-start | bytes 4194304 | tf_op jit(solution)/shard_map/all_to_all | solution.py:391
  252.5 11.6 %collective-permute-start.18 = (bf16[1024,1024]{1,0:T(8,128)(2,1)}, bf16[1024,1024]{1,0:T(8,128)(2,1)S(1)}, u32[]{:S(2)}, u32[]{:S(2)}) collective-permute-start(bf16[1024,1024]{1,0:T(8,128)(2,1)} %get-tuple-element.96), channel_id=1, source_target_pairs={{0,4},{1,5},{2,6},{3,7},{4,0},{5,1},{6,2},{7,3},{8,12},{9,13},{10,... | collective-permute-start | bytes 6291464 | tf_op jit(solution)/shard_map/ppermute | solution.py:317
  252.6 16.1 %collective-permute-start.21 = (bf16[1024,1024]{1,0:T(8,128)(2,1)}, bf16[1024,1024]{1,0:T(8,128)(2,1)S(1)}, u32[]{:S(2)}, u32[]{:S(2)}) collective-permute-start(bf16[1024,1024]{1,0:T(8,128)(2,1)} %get-tuple-element.100), channel_id=1, source_target_pairs={{0,4},{1,5},{2,6},{3,7},{4,0},{5,1},{6,2},{7,3},{8,12},{9,13},{10,... | collective-permute-start | bytes 6291464 | tf_op jit(solution)/shard_map/ppermute | solution.py:317
  264.1 4.7 %copy-start.3 = (bf16[1024,1024]{1,0:T(8,128)(2,1)S(1)}, bf16[1024,1024]{1,0:T(8,128)(2,1)}, u32[]{:S(2)}) copy-start(bf16[1024,1024]{1,0:T(8,128)(2,1)} %get-tuple-element.99) | copy-start | bytes 6291460
  266.8 25.4 %collective-permute-start.19 = (bf16[512,1024]{1,0:T(8,128)(2,1)}, bf16[512,1024]{1,0:T(8,128)(2,1)S(1)}, u32[]{:S(2)}, u32[]{:S(2)}) collective-permute-start(bf16[512,1024]{1,0:T(8,128)(2,1)} %add_convert_fusion.3), channel_id=1, source_target_pairs={{0,1},{1,0},{2,3},{3,2},{4,5},{5,4},{6,7},{7,6},{8,9},{9,8},{10,11... | collective-permute-start | bytes 3145736 | tf_op jit(solution)/shard_map/ppermute | solution.py:317
  281.2 48.7 %collective-permute-start.29 = (bf16[1024,1024]{1,0:T(8,128)(2,1)}, bf16[1024,1024]{1,0:T(8,128)(2,1)}, u32[]{:S(2)}, u32[]{:S(2)}) collective-permute-start(bf16[1024,1024]{1,0:T(8,128)(2,1)} %get-tuple-element.110), channel_id=1, source_target_pairs={{0,16},{1,17},{2,18},{3,19},{4,20},{5,21},{6,22},{7,23},{8,24},{9,... | collective-permute-start | bytes 6291464 | tf_op jit(solution)/shard_map/ppermute | solution.py:317
  281.5 51.6 %collective-permute-start.24 = (bf16[1024,1024]{1,0:T(8,128)(2,1)}, bf16[1024,1024]{1,0:T(8,128)(2,1)}, u32[]{:S(2)}, u32[]{:S(2)}) collective-permute-start(bf16[1024,1024]{1,0:T(8,128)(2,1)} %get-tuple-element.102), channel_id=1, source_target_pairs={{0,8},{1,9},{2,10},{3,11},{4,12},{5,13},{6,14},{7,15},{8,0},{9,1},... | collective-permute-start | bytes 6291464 | tf_op jit(solution)/shard_map/ppermute | solution.py:317
  282.5 43.5 %collective-permute-start.22 = (bf16[512,1024]{1,0:T(8,128)(2,1)}, bf16[512,1024]{1,0:T(8,128)(2,1)}, u32[]{:S(2)}, u32[]{:S(2)}) collective-permute-start(bf16[512,1024]{1,0:T(8,128)(2,1)} %add_convert_fusion.2), channel_id=1, source_target_pairs={{0,1},{1,0},{2,3},{3,2},{4,5},{5,4},{6,7},{7,6},{8,9},{9,8},{10,11... | collective-permute-start | bytes 3145736 | tf_op jit(solution)/shard_map/ppermute | solution.py:317
  295.1 36.5 %collective-permute-start.20 = (bf16[512,1024]{1,0:T(8,128)(2,1)}, bf16[512,1024]{1,0:T(8,128)(2,1)}, u32[]{:S(2)}, u32[]{:S(2)}) collective-permute-start(bf16[512,1024]{1,0:T(8,128)(2,1)} %fusion), channel_id=1, source_target_pairs={{2,4},{3,5},{4,2},{5,3},{10,12},{11,13},{12,10},{13,11},{18,20},{1... | collective-permute-start | bytes 3145736 | tf_op jit(solution)/shard_map/ppermute | solution.py:317
  310.1 19.8 %copy-start.8 = (bf16[1024,1024]{1,0:T(8,128)(2,1)S(1)}, bf16[1024,1024]{1,0:T(8,128)(2,1)}, u32[]{:S(2)}) copy-start(bf16[1024,1024]{1,0:T(8,128)(2,1)} %get-tuple-element.109) | copy-start | bytes 6291460
  327.8 5.3 %copy-start.7 = (bf16[1024,1024]{1,0:T(8,128)(2,1)S(1)}, bf16[1024,1024]{1,0:T(8,128)(2,1)}, u32[]{:S(2)}) copy-start(bf16[1024,1024]{1,0:T(8,128)(2,1)} %get-tuple-element.104) | copy-start | bytes 6291460
  327.8 27.5 %collective-permute-start.23 = (bf16[512,1024]{1,0:T(8,128)(2,1)S(1)}, bf16[512,1024]{1,0:T(8,128)(2,1)S(1)}, u32[]{:S(2)}, u32[]{:S(2)}) collective-permute-start(bf16[512,1024]{1,0:T(8,128)(2,1)S(1)} %fusion.1), channel_id=1, source_target_pairs={{2,4},{3,5},{4,2},{5,3},{10,12},{11,13},{12,10},{13,11},{18,20},{1... | collective-permute-start | bytes 3145736 | tf_op jit(solution)/shard_map/ppermute | solution.py:317
  331.5 3.6 copy-start.4
  331.5 27.2 %collective-permute-start.30 = (bf16[512,1024]{1,0:T(8,128)(2,1)S(1)}, bf16[512,1024]{1,0:T(8,128)(2,1)S(1)}, u32[]{:S(2)}, u32[]{:S(2)}) collective-permute-start(bf16[512,1024]{1,0:T(8,128)(2,1)S(1)} %add_convert_fusion), channel_id=1, source_target_pairs={{0,8},{1,9},{2,10},{3,11},{4,12},{5,13},{6,14},{7,15},{8,0},{9,1},... | collective-permute-start | bytes 3145736 | tf_op jit(solution)/shard_map/ppermute | solution.py:317
  334.8 31.9 %collective-permute-start.25 = (bf16[512,1024]{1,0:T(8,128)(2,1)S(1)}, bf16[512,1024]{1,0:T(8,128)(2,1)S(1)}, u32[]{:S(2)}, u32[]{:S(2)}) collective-permute-start(bf16[512,1024]{1,0:T(8,128)(2,1)S(1)} %add_convert_fusion.1), channel_id=1, source_target_pairs={{0,16},{1,17},{2,18},{3,19},{4,20},{5,21},{6,22},{7,23},{8,24},{9,... | collective-permute-start | bytes 3145736 | tf_op jit(solution)/shard_map/ppermute | solution.py:317
  361.7 15.8 %collective-permute-start.32 = (bf16[256,1024]{1,0:T(8,128)(2,1)S(1)}, bf16[256,1024]{1,0:T(8,128)(2,1)S(1)}, u32[]{:S(2)}, u32[]{:S(2)}) collective-permute-start(bf16[256,1024]{1,0:T(8,128)(2,1)S(1)} %get-tuple-element.112), channel_id=1, source_target_pairs={{2,0},{3,1},{4,2},{5,3},{10,8},{11,9},{12,10},{13,11},{18,16},{19,... | collective-permute-start | bytes 1572872 | tf_op jit(solution)/shard_map/ppermute | solution.py:317
  363.4 36.1 %collective-permute-start.33 = (bf16[256,1024]{1,0:T(8,128)(2,1)}, bf16[256,1024]{1,0:T(8,128)(2,1)S(1)}, u32[]{:S(2)}, u32[]{:S(2)}) collective-permute-start(bf16[256,1024]{1,0:T(8,128)(2,1)} %get-tuple-element.113), channel_id=1, source_target_pairs={{2,4},{3,5},{4,6},{5,7},{10,12},{11,13},{12,14},{13,15},{18,20},{1... | collective-permute-start | bytes 1572872 | tf_op jit(solution)/shard_map/ppermute | solution.py:317
  365.4 34.2 %collective-permute-start.31 = (bf16[256,1024]{1,0:T(8,128)(2,1)}, bf16[256,1024]{1,0:T(8,128)(2,1)}, u32[]{:S(2)}, u32[]{:S(2)}) collective-permute-start(bf16[256,1024]{1,0:T(8,128)(2,1)} %get-tuple-element.124), channel_id=1, source_target_pairs={{0,4},{1,5},{6,2},{7,3},{8,12},{9,13},{14,10},{15,11},{16,20},{17,... | collective-permute-start | bytes 1572872 | tf_op jit(solution)/shard_map/ppermute | solution.py:317
  366.7 12.3 %copy-start = (f32[1,512,2048]{2,1,0:T(8,128)S(1)}, f32[1,512,2048]{2,1,0:T(8,128)}, u32[]{:S(2)}) copy-start(f32[1,512,2048]{2,1,0:T(8,128)} %param.12) | copy-start | bytes 12582916
  369.9 31.1 %collective-permute-start.27 = (bf16[256,1024]{1,0:T(8,128)(2,1)}, bf16[256,1024]{1,0:T(8,128)(2,1)}, u32[]{:S(2)}, u32[]{:S(2)}) collective-permute-start(bf16[256,1024]{1,0:T(8,128)(2,1)} %get-tuple-element.107), channel_id=1, source_target_pairs={{2,0},{3,1},{4,2},{5,3},{10,8},{11,9},{12,10},{13,11},{18,16},{19,... | collective-permute-start | bytes 1572872 | tf_op jit(solution)/shard_map/ppermute | solution.py:317
  375.3 35.6 %collective-permute-start.28 = (bf16[256,1024]{1,0:T(8,128)(2,1)}, bf16[256,1024]{1,0:T(8,128)(2,1)}, u32[]{:S(2)}, u32[]{:S(2)}) collective-permute-start(bf16[256,1024]{1,0:T(8,128)(2,1)} %get-tuple-element.108), channel_id=1, source_target_pairs={{2,4},{3,5},{4,6},{5,7},{10,12},{11,13},{12,14},{13,15},{18,20},{1... | collective-permute-start | bytes 1572872 | tf_op jit(solution)/shard_map/ppermute | solution.py:317
  377.4 33.4 %collective-permute-start.26 = (bf16[256,1024]{1,0:T(8,128)(2,1)}, bf16[256,1024]{1,0:T(8,128)(2,1)}, u32[]{:S(2)}, u32[]{:S(2)}) collective-permute-start(bf16[256,1024]{1,0:T(8,128)(2,1)} %get-tuple-element.121), channel_id=1, source_target_pairs={{0,4},{1,5},{6,2},{7,3},{8,12},{9,13},{14,10},{15,11},{16,20},{17,... | collective-permute-start | bytes 1572872 | tf_op jit(solution)/shard_map/ppermute | solution.py:317
  401.0 11.7 %copy-start.2 = (f32[1,256,2048]{2,1,0:T(8,128)S(1)}, f32[1,256,2048]{2,1,0:T(8,128)}, u32[]{:S(2)}) copy-start(f32[1,256,2048]{2,1,0:T(8,128)} %param.13) | copy-start | bytes 6291460
  401.0 11.7 %copy-start.6 = (f32[1,256,2048]{2,1,0:T(8,128)S(1)}, f32[1,256,2048]{2,1,0:T(8,128)}, u32[]{:S(2)}) copy-start(f32[1,256,2048]{2,1,0:T(8,128)} %param.15) | copy-start | bytes 6291460
  (5 other events, 6.0 us)
